TPU v7x, 256 devices: a whole 4x4x8 slice. The times are simulated.
256 devices in a mesh: ctx: 32 (over z, x_lo, core), head: 8 (over x_hi, y).
Axes of the slice: x: 4 (x_hi: 2, x_lo: 2; x = x_hi * 2 + x_lo), y: 4, z: 8, core: 2. Of those that a mesh axis runs over, the one named last changes fastest.
Arguments:
- queries: bfloat16 [32768, 3072], P(('ctx', 'head')), may hold values from -48 to 48
- key_rows: bfloat16 [32768, 3072], P(('ctx', 'head')), may hold values from -6 to 6
- value_rows: bfloat16 [32768, 3072], P(('ctx', 'head')), may hold values from -6 to 6
- out_cotangent: bfloat16 [32768, 3072], P(('ctx', 'head')), may hold values from -6 to 6
- gate_table: float32 [128, 3072], replicated, may hold values from -6 to 6
- span_ids: int32 [32768], replicated, may hold values from 0 to 191, never falling along the last dimension, each value on 1 to 256 neighbouring positions
- noise_level: int32 [192], replicated, may hold values from 0 to 127
- block_mask: int32 [192, 192], replicated, may hold values from 0 to 1, as said below
Outputs:
- mixed_out: bfloat16 [32768, 3072], P(('ctx', 'head'))
- query_grad: bfloat16 [32768, 3072], P(('ctx', 'head'))
- key_grad: bfloat16 [32768, 3072], P(('ctx', 'head'))
- value_grad: bfloat16 [32768, 3072], P(('ctx', 'head'))
- gate_grad: float32 [128, 3072], replicated
Inputs may be any that keep to these rules, and one draw needn't show every extreme that they name: `span_ids`: span ids never fall along the tokens; every span holds 1 to 256 tokens, one span exactly 256. `block_mask`: entries are 0 or 1; entries [c, c] and [c, c - 1] are 1 for every span c.
All inputs are finite; a program needn't handle non-finite values.
Results may differ from a plain program's by a relative error of at most 0.023.
Values may be sent and summed in bfloat16 or wider, within the bound.
A program may use at most 128 MiB of HBM per device.

v0:
```python
import math

import jax
import jax.numpy as jnp
from jax import lax
from jax.sharding import PartitionSpec as P

DH = 128
SPAN = 256


def with_halo(cells, sides, width):
    for axis, dim in sides:
        count = lax.axis_size(axis)
        ends = count - 1
        head = lax.slice_in_dim(cells, 0, width, axis=dim)
        tail = lax.slice_in_dim(cells, cells.shape[dim] - width, cells.shape[dim], axis=dim)
        cells = jnp.concatenate(
            [
                lax.ppermute(tail, axis, [(i, (i + 1) % count) for i in range(ends)]),
                cells,
                lax.ppermute(head, axis, [((i + 1) % count, i) for i in range(ends)]),
            ],
            axis=dim,
        )
    return cells


def from_behind(shard, axis, by):
    peers = lax.axis_size(axis)
    pairs = [(i, i + by) for i in range(peers) if 0 <= i + by < peers]
    return lax.ppermute(shard, axis, pairs)


def attend(q_block, k_block, v_block, g_block, visible):
    count_q = q_block.shape[0]
    count_k = k_block.shape[0]
    head_count = q_block.shape[1] // DH
    score_scale = 1.0 / math.sqrt(DH)
    q_heads = q_block.reshape(count_q, head_count, DH)
    k_heads = k_block.reshape(count_k, head_count, DH)
    v_heads = v_block.reshape(count_k, head_count, DH)
    g_heads = g_block.reshape(count_q, head_count, DH)
    scores = (
        jnp.einsum("qhd,khd->hqk", q_heads, k_heads, preferred_element_type=jnp.float32)
        * score_scale
    )
    scores = jnp.where(visible[None], scores, -jnp.inf)
    row_max = jnp.max(scores, axis=2, keepdims=True)
    log_total = row_max + jnp.log(jnp.sum(jnp.exp(scores - row_max), axis=2, keepdims=True))
    attention = jnp.exp(scores - log_total)
    attention_low = attention.astype(jnp.bfloat16)
    attended = jnp.einsum(
        "hqk,khd->qhd", attention_low, v_heads, preferred_element_type=jnp.float32
    ).astype(jnp.bfloat16)
    row_dot = jnp.einsum("qhd,qhd->hq", g_heads, attended, preferred_element_type=jnp.float32)[
        :, :, None
    ]
    prob_grad = jnp.einsum("qhd,khd->hqk", g_heads, v_heads, preferred_element_type=jnp.float32)
    score_grad = (attention * (prob_grad - row_dot)).astype(jnp.bfloat16)
    query_grad = (
        jnp.einsum("hqk,khd->qhd", score_grad, k_heads, preferred_element_type=jnp.float32)
        * score_scale
    ).astype(jnp.bfloat16)
    key_grad = (
        jnp.einsum("hqk,qhd->khd", score_grad, q_heads, preferred_element_type=jnp.float32)
        * score_scale
    )
    value_grad = jnp.einsum(
        "hqk,qhd->khd", attention_low, g_heads, preferred_element_type=jnp.float32
    )
    return (
        attended.reshape(count_q, -1),
        query_grad.reshape(count_q, -1),
        key_grad.reshape(count_k, -1),
        value_grad.reshape(count_k, -1),
    )


def per_device(
    queries, key_rows, value_rows, out_cotangent, gate_table, span_ids, noise_level, block_mask
):
    head_groups = lax.axis_size("head")
    tok_rows = queries.shape[0]
    full_width = queries.shape[1]
    local_width = full_width // head_groups
    ctx_tokens = tok_rows * head_groups
    ctx_pos = lax.axis_index("ctx")
    head_pos = lax.axis_index("head")
    span_total = noise_level.shape[0]
    level_count = gate_table.shape[0]
    total_tokens = span_ids.shape[0]
    span_range = jnp.arange(span_total, dtype=jnp.int32)
    level_range = jnp.arange(level_count, dtype=jnp.int32)
    ctx_start = ctx_pos * ctx_tokens
    query_span = lax.dynamic_slice_in_dim(span_ids, ctx_start, ctx_tokens, 0)
    own_span = lax.dynamic_slice_in_dim(span_ids, ctx_start + head_pos * tok_rows, tok_rows, 0)
    level_onehot = (
        jnp.sum(
            jnp.where(own_span[:, None] == span_range[None, :], noise_level[None, :], 0), axis=1
        )[:, None]
        == level_range[None, :]
    ).astype(jnp.float32)
    gate_rows = jnp.dot(level_onehot, gate_table, precision=lax.Precision.HIGHEST)
    sent_grad = (gate_rows * out_cotangent.astype(jnp.float32)).astype(jnp.bfloat16)
    query_local, key_local, value_local, grad_local = (
        lax.all_to_all(queries, "head", split_axis=1, concat_axis=0, tiled=True),
        lax.all_to_all(key_rows, "head", split_axis=1, concat_axis=0, tiled=True),
        lax.all_to_all(value_rows, "head", split_axis=1, concat_axis=0, tiled=True),
        lax.all_to_all(sent_grad, "head", split_axis=1, concat_axis=0, tiled=True),
    )
    key_pairs = jnp.stack([key_local, value_local])
    widened = with_halo(key_pairs, (("ctx", 1),), ctx_tokens)
    buffer = widened[:, : 2 * ctx_tokens + SPAN]
    buffer_len = 2 * ctx_tokens + SPAN
    key_pos = ctx_start - ctx_tokens + jnp.arange(buffer_len, dtype=jnp.int32)
    key_span = jnp.take(span_ids, jnp.clip(key_pos, 0, total_tokens - 1))
    key_valid = (key_pos >= 0) & (key_pos < total_tokens)
    query_pos = ctx_start + jnp.arange(ctx_tokens, dtype=jnp.int32)
    q_size = min(512, ctx_tokens)
    k_size = ctx_tokens + q_size + SPAN
    mask_low = block_mask.astype(jnp.bfloat16)

    def one_block(partials, offset):
        q_block = lax.dynamic_slice_in_dim(query_local, offset, q_size, 0)
        g_block = lax.dynamic_slice_in_dim(grad_local, offset, q_size, 0)
        key_slab = lax.dynamic_slice_in_dim(buffer, offset, k_size, 1)
        span_q = lax.dynamic_slice_in_dim(query_span, offset, q_size, 0)
        pos_q = lax.dynamic_slice_in_dim(query_pos, offset, q_size, 0)
        span_k = lax.dynamic_slice_in_dim(key_span, offset, k_size, 0)
        pos_k = lax.dynamic_slice_in_dim(key_pos, offset, k_size, 0)
        valid_k = lax.dynamic_slice_in_dim(key_valid, offset, k_size, 0)
        mask_rows = jnp.take(mask_low, span_q, axis=0)
        onehot_k = (span_range[:, None] == span_k[None, :]).astype(jnp.bfloat16)
        allowed = jnp.dot(mask_rows, onehot_k, preferred_element_type=jnp.float32) > 0.5
        visible = (
            allowed
            & (span_k[None, :] <= span_q[:, None])
            & (pos_q[:, None] - pos_k[None, :] < ctx_tokens)
            & valid_k[None, :]
        )
        attended, query_grad, key_grad, value_grad = attend(
            q_block, key_slab[0], key_slab[1], g_block, visible
        )
        window_part = lax.dynamic_slice_in_dim(partials, offset, k_size, 1) + jnp.stack(
            [key_grad, value_grad]
        )
        partials = lax.dynamic_update_slice_in_dim(partials, window_part, offset, 1)
        return (partials, (attended, query_grad))

    offsets = jnp.arange(0, ctx_tokens, q_size, dtype=jnp.int32)
    empty_grads = jnp.zeros((2, buffer_len, local_width), jnp.float32)
    key_partials, (attended, query_grad_local) = lax.scan(one_block, empty_grads, offsets)
    attended = attended.reshape(ctx_tokens, local_width)
    query_grad_local = query_grad_local.reshape(ctx_tokens, local_width)
    from_later = from_behind(key_partials[:, :ctx_tokens], "ctx", -1)
    from_earlier = from_behind(
        key_partials[:, 2 * ctx_tokens :].astype(jnp.bfloat16), "ctx", 1
    ).astype(jnp.float32)
    own_grads = key_partials[:, ctx_tokens : 2 * ctx_tokens] + from_later
    own_grads = own_grads.at[:, :SPAN].add(from_earlier)
    key_grad_local = own_grads[0].astype(jnp.bfloat16)
    value_grad_local = own_grads[1].astype(jnp.bfloat16)
    first_back, query_grad, key_grad, value_grad = (
        lax.all_to_all(attended, "head", split_axis=0, concat_axis=1, tiled=True),
        lax.all_to_all(query_grad_local, "head", split_axis=0, concat_axis=1, tiled=True),
        lax.all_to_all(key_grad_local, "head", split_axis=0, concat_axis=1, tiled=True),
        lax.all_to_all(value_grad_local, "head", split_axis=0, concat_axis=1, tiled=True),
    )
    mixed_out = (gate_rows * first_back.astype(jnp.float32)).astype(jnp.bfloat16)
    products = out_cotangent.astype(jnp.float32) * first_back.astype(jnp.float32)
    gate_part = jnp.dot(level_onehot.T, products, precision=lax.Precision.HIGHEST)
    gate_grad = lax.psum(gate_part, ("ctx", "head"))
    return (mixed_out, query_grad, key_grad, value_grad, gate_grad)


def solution(mesh):
    return jax.shard_map(
        per_device,
        mesh=mesh,
        in_specs=(
            P(("ctx", "head"), None),
            P(("ctx", "head"), None),
            P(("ctx", "head"), None),
            P(("ctx", "head"), None),
            P(),
            P(),
            P(),
            P(),
        ),
        out_specs=(
            P(("ctx", "head"), None),
            P(("ctx", "head"), None),
            P(("ctx", "head"), None),
            P(("ctx", "head"), None),
            P(),
        ),
        check_vma=False,
    )
```

profile of v0, /device:TPU:1, one launch (start us, length us, event | category | flops | bytes accessed | tf_op | source)
XLA Modules:
  0.0 671.2 jit_solution(7422589316621752729)
XLA Ops:
  7.2 2.4 copy.100
  9.6 7.5 %all-to-all-start.2 = ((bf16[128,8,384]{0,2,1:T(8,128)(2,1)}), bf16[128,8,384]{0,2,1:T(8,128)(2,1)S(1)}, u32[]{:S(2)}, u32[]{:S(2)}) async-start(bf16[128,8,384]{0,2,1:T(8,128)(2,1)} %bitcast.8), calls=%async_computation.2 | async-start | bytes 1572864 | tf_op jit(solution)/shard_map/all_to_all | solution.py:109
  18.3 10.2 %all-to-all-done.2 = bf16[128,8,384]{0,2,1:T(8,128)(2,1)S(1)} async-done(((bf16[128,8,384]{0,2,1:T(8,128)(2,1)}), bf16[128,8,384]{0,2,1:T(8,128)(2,1)S(1)}, u32[]{:S(2)}, u32[]{:S(2)}) %all-to-all-start.2) | async-done | bytes 786464 | tf_op jit(solution)/shard_map/all_to_all | solution.py:109
  28.5 5.9 all-to-all-start.1
  34.8 10.9 %all-to-all-done.1 = bf16[128,8,384]{0,2,1:T(8,128)(2,1)} async-done(((bf16[128,8,384]{0,2,1:T(8,128)(2,1)}), bf16[128,8,384]{0,2,1:T(8,128)(2,1)}, u32[]{:S(2)}, u32[]{:S(2)}) %all-to-all-start.1) | async-done | bytes 786464 | tf_op jit(solution)/shard_map/all_to_all | solution.py:108
  48.5 5.3 collective-permute-start
  58.3 4.2 all-to-all-start
  63.3 3.3 fusion.16
  67.7 32.9 %all-to-all-done = bf16[128,8,384]{0,2,1:T(8,128)(2,1)} async-done(((bf16[128,8,384]{0,2,1:T(8,128)(2,1)}), bf16[128,8,384]{0,2,1:T(8,128)(2,1)}, u32[]{:S(2)}, u32[]{:S(2)}) %all-to-all-start) | async-done | bytes 786464 | tf_op jit(solution)/shard_map/all_to_all | solution.py:107
  100.6 3.8 all-to-all-start.3
  104.4 12.3 %gather_fusion.1 = s32[2304]{0:T(1024)S(1)} fusion(s32[32768]{0:T(1024)S(1)} %copy-done.3, s32[3072]{0:T(1024)S(1)} %pad_clamp_fusion.1), kind=kCustom, calls=%fused_computation.1 | custom fusion | bytes 27648 | tf_op jit(solution)/shard_map/jit(_take)/gather | solution.py:117
  119.1 6.9 %pad_maximum_fusion = bf16[2,2304,384]{2,1,0:T(8,128)(2,1)} fusion(bf16[2,1024,384]{2,1,0:T(8,128)(2,1)} %collective-permute-done.1, bf16[2,1024,384]{2,1,0:T(8,128)(2,1)} %collective-permute-done, bf16[1,1024,384]{2,1,0:T(8,128)(2,1)S(1)} %bitcast.130, bf16[1,1024,384]{2,1,0:T(8,128)(2,1)S(1)} %bitcast.132), kind=kLoop, calls=%fused_computation.36 | loop fusion | flops 14155776 | bytes 8257536 | tf_op jit(solution)/shard_map/concatenate | solution.py:18
  126.0 3.4 broadcast_in_dim.70
  129.4 173.5 %while.16 = (s32[]{:T(128)}, f32[2,2304,384]{1,2,0:T(8,128)}, bf16[2,512,384]{2,1,0:T(8,128)(2,1)}, bf16[2,512,384]{2,1,0:T(8,128)(2,1)}, s32[2]{0:T(128)S(1)}, ...) while((s32[]{:T(128)}, f32[2,2304,384]{1,2,0:T(8,128)}, ...), condition=%wide.region_4.5_spmd.clone, body=%wide.region_1.4_spmd.clone.sunk | while | flops 4649667072 | bytes 238628176 | solution.py:153
  137.2 4.0 constant_dynamic-slice_fusion.9
  144.2 2.5 fusion.72
  146.7 3.2 exponential_reduce_fusion.2
  150.9 2.5 copy.150
  155.5 8.6 %fusion.74 = (f32[3,512]{1,0:T(4,128)S(1)}, bf16[3,128,512]{2,1,0:T(8,128)(2,1)}) fusion(bf16[3,512,128]{1,2,0:T(8,128)(2,1)} %bitcast.123, bf16[1792,3,128]{0,2,1:T(8,128)(2,1)} %bitcast.119, f32[3,512,1792]{2,1,0:T(8,128)} %copy-done.2, f32[3,512]{1,0:T(4,128)S(1)} %log_add_fusion.2, pred[512,1792]{1,0:T(8,128)(4,1)S(1)} %fusion.71), kind=kOutput, calls=%fused_computation.19.clone.1 | convolution fusion | flops 716634624 | bytes 14102528 | tf_op jit(solution)/shard_map/while/body/eval_jaxpr/hqk,khd->qhd/dot_general | solution.py:53
  164.1 6.6 multiply_convert_fusion.3
  170.7 2.4 copy-done.4
  177.4 3.5 convolution_multiply_fusion.3
  180.9 6.1 fusion.73
  187.2 3.9 maximum_add_fusion.2
  191.1 25.3 %dynamic_update_slice.18 = f32[2,2304,384]{1,2,0:T(8,128)} dynamic-update-slice(f32[2,2304,384]{1,2,0:T(8,128)} %get-tuple-element.360, f32[2,1792,384]{1,2,0:T(8,128)} %maximum_add_fusion.2, s32[]{:T(128)} %constant.99.clone.1..sunk, s32[]{:T(128)S(6)} %select_n.121, s32[]{:T(128)} %constant.99.clone.1..sunk) | dynamic-update-slice | bytes 11010052 | tf_op jit(solution)/shard_map/while/body/eval_jaxpr/dynamic_update_slice | solution.py:148
  224.2 4.0 constant_dynamic-slice_fusion.9
  231.3 2.5 fusion.72
  233.7 3.2 exponential_reduce_fusion.2
  237.9 2.5 copy.150
  242.5 8.6 %fusion.74 = (f32[3,512]{1,0:T(4,128)S(1)}, bf16[3,128,512]{2,1,0:T(8,128)(2,1)}) fusion(bf16[3,512,128]{1,2,0:T(8,128)(2,1)} %bitcast.123, bf16[1792,3,128]{0,2,1:T(8,128)(2,1)} %bitcast.119, f32[3,512,1792]{2,1,0:T(8,128)} %copy-done.2, f32[3,512]{1,0:T(4,128)S(1)} %log_add_fusion.2, pred[512,1792]{1,0:T(8,128)(4,1)S(1)} %fusion.71), kind=kOutput, calls=%fused_computation.19.clone.1 | convolution fusion | flops 716634624 | bytes 14102528 | tf_op jit(solution)/shard_map/while/body/eval_jaxpr/hqk,khd->qhd/dot_general | solution.py:53
  251.1 6.6 multiply_convert_fusion.3
  264.4 3.5 convolution_multiply_fusion.3
  267.9 6.1 fusion.73
  274.2 3.9 maximum_add_fusion.2
  278.1 24.8 %dynamic_update_slice.18 = f32[2,2304,384]{1,2,0:T(8,128)} dynamic-update-slice(f32[2,2304,384]{1,2,0:T(8,128)} %get-tuple-element.360, f32[2,1792,384]{1,2,0:T(8,128)} %maximum_add_fusion.2, s32[]{:T(128)} %constant.99.clone.1..sunk, s32[]{:T(128)S(6)} %select_n.121, s32[]{:T(128)} %constant.99.clone.1..sunk) | dynamic-update-slice | bytes 11010052 | tf_op jit(solution)/shard_map/while/body/eval_jaxpr/dynamic_update_slice | solution.py:148
  302.9 4.0 slice.53
  308.8 6.6 all-to-all-start.4
  316.6 3.3 collective-permute-start.3
  319.9 25.7 %all-to-all-done.4 = bf16[8,128,384]{2,1,0:T(8,128)(2,1)S(1)} async-done(((bf16[8,128,384]{2,1,0:T(8,128)(2,1)}), bf16[8,128,384]{2,1,0:T(8,128)(2,1)S(1)}, u32[]{:S(2)}, u32[]{:S(2)}) %all-to-all-start.4) | async-done | bytes 786464 | tf_op jit(solution)/shard_map/all_to_all | solution.py:165
  345.6 3.9 all-to-all-start.5
  350.4 3.8 slice_add_fusion
  356.8 4.4 all-to-all-done.5
  361.2 5.6 all-to-all-start.6
  369.5 2.4 copy.109
  378.1 6.1 all-to-all-start.7
  388.0 7.5 %all-to-all-done.7 = bf16[8,128,384]{2,1,0:T(8,128)(2,1)} async-done(((bf16[8,128,384]{2,1,0:T(8,128)(2,1)}), bf16[8,128,384]{2,1,0:T(8,128)(2,1)}, u32[]{:S(2)}, u32[]{:S(2)}) %all-to-all-start.7) | async-done | bytes 786464 | tf_op jit(solution)/shard_map/all_to_all | solution.py:168
  398.2 263.4 %all-reduce.2.cloned.1.call-done = f32[128,3072]{1,0:T(8,128)} async-done(((f32[128,3072]{1,0:T(8,128)}), f32[128,3072]{1,0:T(8,128)}) %all-reduce.2.cloned.1.call-update) | async-done | bytes 1572880 | tf_op jit(solution)/shard_map/psum | solution.py:173
  661.6 2.7 copy.170
  (148 shorter events, 68.2 us)
Async XLA Ops:
  7.2 56.2 %copy-start = (f32[128,3072]{1,0:T(8,128)S(1)}, f32[128,3072]{1,0:T(8,128)}, u32[]{:S(2)}) copy-start(f32[128,3072]{1,0:T(8,128)} %param.16) | copy-start | bytes 4718596
  7.2 9.9 %copy-start.15 = (bf16[128,3072]{1,0:T(8,128)(2,1)S(1)}, bf16[128,3072]{1,0:T(8,128)(2,1)}, u32[]{:S(2)}) copy-start(bf16[128,3072]{1,0:T(8,128)(2,1)} %param.13) | copy-start | bytes 2359300
  9.6 18.9 %all-to-all-start.2 = ((bf16[128,8,384]{0,2,1:T(8,128)(2,1)}), bf16[128,8,384]{0,2,1:T(8,128)(2,1)S(1)}, u32[]{:S(2)}, u32[]{:S(2)}) async-start(bf16[128,8,384]{0,2,1:T(8,128)(2,1)} %bitcast.8), calls=%async_computation.2 | async-start | bytes 1572864 | tf_op jit(solution)/shard_map/all_to_all | solution.py:109
  28.5 17.2 %all-to-all-start.1 = ((bf16[128,8,384]{0,2,1:T(8,128)(2,1)}), bf16[128,8,384]{0,2,1:T(8,128)(2,1)}, u32[]{:S(2)}, u32[]{:S(2)}) async-start(bf16[128,8,384]{0,2,1:T(8,128)(2,1)} %bitcast.5), calls=%async_computation.1 | async-start | bytes 1572864 | tf_op jit(solution)/shard_map/all_to_all | solution.py:108
  34.8 27.8 %copy-start.3 = (s32[32768]{0:T(1024)S(1)}, s32[32768]{0:T(1024)}, u32[]{:S(2)}) copy-start(s32[32768]{0:T(1024)} %param.17) | copy-start | bytes 393220
  34.8 27.8 %copy-start.19 = (s32[192]{0:T(256)S(1)}, s32[192]{0:T(256)}, u32[]{:S(2)}) copy-start(s32[192]{0:T(256)} %param.18) | copy-start | bytes 2308
  48.5 70.5 %collective-permute-start = (bf16[2,1024,384]{2,1,0:T(8,128)(2,1)}, bf16[2,1024,384]{2,1,0:T(8,128)(2,1)}, u32[]{:S(2)}, u32[]{:S(2)}) collective-permute-start(bf16[2,1024,384]{2,1,0:T(8,128)(2,1)} %pad_maximum_fusion.3), channel_id=1, source_target_pairs={{0,8},{8,16},{16,24},{24,32},{32,40},{40,48},{48,56},{56,64},{64,7... | collective-permute-start | bytes 4718600 | tf_op jit(solution)/shard_map/ppermute | solution.py:20
  53.8 65.3 %collective-permute-start.1 = (bf16[2,1024,384]{2,1,0:T(8,128)(2,1)}, bf16[2,1024,384]{2,1,0:T(8,128)(2,1)}, u32[]{:S(2)}, u32[]{:S(2)}) collective-permute-start(bf16[2,1024,384]{2,1,0:T(8,128)(2,1)} %pad_maximum_fusion.3), channel_id=1, source_target_pairs={{8,0},{16,8},{24,16},{32,24},{40,32},{48,40},{56,48},{64,56},{72,6... | collective-permute-start | bytes 4718600 | tf_op jit(solution)/shard_map/ppermute | solution.py:22
  58.3 42.3 %all-to-all-start = ((bf16[128,8,384]{0,2,1:T(8,128)(2,1)}), bf16[128,8,384]{0,2,1:T(8,128)(2,1)}, u32[]{:S(2)}, u32[]{:S(2)}) async-start(bf16[128,8,384]{0,2,1:T(8,128)(2,1)} %bitcast.136), calls=%async_computation | async-start | bytes 1572864 | tf_op jit(solution)/shard_map/all_to_all | solution.py:107
  62.7 0.6 copy-start.17
  100.6 25.4 %all-to-all-start.3 = ((bf16[128,8,384]{2,0,1:T(8,128)(2,1)}), bf16[128,8,384]{2,0,1:T(8,128)(2,1)S(1)}, u32[]{:S(2)}, u32[]{:S(2)}) async-start(bf16[128,8,384]{2,0,1:T(8,128)(2,1)} %bitcast.134), calls=%async_computation.3 | async-start | bytes 1572864 | tf_op jit(solution)/shard_map/all_to_all | solution.py:110
  104.4 12.3 %copy-start.16 = (s32[192,192]{1,0:T(8,128)S(1)}, s32[192,192]{1,0:T(8,128)}, u32[]{:S(2)}) copy-start(s32[192,192]{1,0:T(8,128)} %param.19) | copy-start | bytes 442372
  126.0 3.4 dynamic-slice-start
  129.4 7.8 %copy-start.8 = (bf16[1024,384]{1,0:T(8,128)(2,1)}, bf16[1024,384]{1,0:T(8,128)(2,1)S(1)}, u32[]{:S(2)}) copy-start(bf16[1024,384]{1,0:T(8,128)(2,1)S(1)} %get-tuple-element.391) | copy-start | bytes 2359300 | tf_op jit(solution)/shard_map/while
  146.7 4.2 copy-start.2
  155.5 8.6 %copy-start.5 = (bf16[1,1792,384]{1,2,0:T(8,128)(2,1)S(1)}, bf16[1,1792,384]{1,2,0:T(8,128)(2,1)}, u32[]{:S(2)}) copy-start(bf16[1,1792,384]{1,2,0:T(8,128)(2,1)} %copy.150) | copy-start | bytes 4128772 | tf_op jit(solution)/shard_map/while
  155.5 8.6 %copy-start.6 = (bf16[512,384]{0,1:T(8,128)(2,1)S(1)}, bf16[512,384]{0,1:T(8,128)(2,1)}, u32[]{:S(2)}) copy-start(bf16[512,384]{0,1:T(8,128)(2,1)} %copy.147) | copy-start | bytes 1179652 | tf_op jit(solution)/shard_map/while
  170.7 2.4 copy-start.4
  177.4 3.5 copy-start.7
  180.9 6.2 slice-start
  180.9 6.3 slice-start.1
  191.1 25.3 %copy-start.9 = (bf16[1024,384]{1,0:T(8,128)(2,1)S(1)}, bf16[1024,384]{1,0:T(8,128)(2,1)}, u32[]{:S(2)}) copy-start(bf16[1024,384]{1,0:T(8,128)(2,1)} %copy-done.8) | copy-start | bytes 2359300 | tf_op jit(solution)/shard_map/while
  216.4 7.8 %copy-start.8 = (bf16[1024,384]{1,0:T(8,128)(2,1)}, bf16[1024,384]{1,0:T(8,128)(2,1)S(1)}, u32[]{:S(2)}) copy-start(bf16[1024,384]{1,0:T(8,128)(2,1)S(1)} %get-tuple-element.391) | copy-start | bytes 2359300 | tf_op jit(solution)/shard_map/while
  233.7 4.2 copy-start.2
  242.5 8.6 %copy-start.5 = (bf16[1,1792,384]{1,2,0:T(8,128)(2,1)S(1)}, bf16[1,1792,384]{1,2,0:T(8,128)(2,1)}, u32[]{:S(2)}) copy-start(bf16[1,1792,384]{1,2,0:T(8,128)(2,1)} %copy.150) | copy-start | bytes 4128772 | tf_op jit(solution)/shard_map/while
  242.5 8.6 %copy-start.6 = (bf16[512,384]{0,1:T(8,128)(2,1)S(1)}, bf16[512,384]{0,1:T(8,128)(2,1)}, u32[]{:S(2)}) copy-start(bf16[512,384]{0,1:T(8,128)(2,1)} %copy.147) | copy-start | bytes 1179652 | tf_op jit(solution)/shard_map/while
  257.7 2.4 copy-start.4
  264.4 3.5 copy-start.7
  267.9 6.2 slice-start
  267.9 6.3 slice-start.1
  278.1 24.8 %copy-start.9 = (bf16[1024,384]{1,0:T(8,128)(2,1)S(1)}, bf16[1024,384]{1,0:T(8,128)(2,1)}, u32[]{:S(2)}) copy-start(bf16[1024,384]{1,0:T(8,128)(2,1)} %copy-done.8) | copy-start | bytes 2359300 | tf_op jit(solution)/shard_map/while
  306.9 43.5 %collective-permute-start.2 = (f32[2,1024,384]{1,2,0:T(8,128)}, f32[2,1024,384]{1,2,0:T(8,128)}, u32[]{:S(2)}, u32[]{:S(2)}) collective-permute-start(f32[2,1024,384]{1,2,0:T(8,128)} %slice.53), channel_id=1, source_target_pairs={{8,0},{16,8},{24,16},{32,24},{40,32},{48,40},{56,48},{64,56},{72,6... | collective-permute-start | bytes 9437192 | tf_op jit(solution)/shard_map/ppermute | solution.py:32
  308.8 36.8 %all-to-all-start.4 = ((bf16[8,128,384]{2,1,0:T(8,128)(2,1)}), bf16[8,128,384]{2,1,0:T(8,128)(2,1)S(1)}, u32[]{:S(2)}, u32[]{:S(2)}) async-start(bf16[8,128,384]{2,1,0:T(8,128)(2,1)} %bitcast.13), calls=%async_computation.4 | async-start | bytes 1572864 | tf_op jit(solution)/shard_map/all_to_all | solution.py:165
  316.6 37.6 %collective-permute-start.3 = (bf16[2,256,384]{1,2,0:T(8,128)(2,1)S(1)}, bf16[2,256,384]{1,2,0:T(8,128)(2,1)S(1)}, u32[]{:S(2)}, u32[]{:S(2)}) collective-permute-start(bf16[2,256,384]{1,2,0:T(8,128)(2,1)S(1)} %slice.73), channel_id=1, source_target_pairs={{0,8},{8,16},{16,24},{24,32},{32,40},{40,48},{48,56},{56,64},{64,7... | collective-permute-start | bytes 1179656 | tf_op jit(solution)/shard_map/ppermute | solution.py:32
  345.6 8.6 %copy-start.13 = (bf16[8,128,384]{2,1,0:T(8,128)(2,1)}, bf16[8,128,384]{2,1,0:T(8,128)(2,1)S(1)}, u32[]{:S(2)}) copy-start(bf16[8,128,384]{2,1,0:T(8,128)(2,1)S(1)} %all-to-all-done.4) | copy-start | bytes 2359300
  345.6 15.6 %all-to-all-start.5 = ((bf16[8,128,384]{2,1,0:T(8,128)(2,1)}), bf16[8,128,384]{2,1,0:T(8,128)(2,1)S(1)}, u32[]{:S(2)}, u32[]{:S(2)}) async-start(bf16[8,128,384]{2,1,0:T(8,128)(2,1)} %bitcast.15), calls=%async_computation.5 | async-start | bytes 1572864 | tf_op jit(solution)/shard_map/all_to_all | solution.py:166
  355.7 11.2 %copy-start.14 = (bf16[8,128,384]{2,1,0:T(8,128)(2,1)S(1)}, bf16[8,128,384]{2,1,0:T(8,128)(2,1)}, u32[]{:S(2)}) copy-start(bf16[8,128,384]{2,1,0:T(8,128)(2,1)} %copy-done.13) | copy-start | bytes 2359300
  356.8 10.3 %copy-start.11 = (bf16[128,3072]{1,0:T(8,128)(2,1)S(1)}, bf16[128,3072]{1,0:T(8,128)(2,1)}, u32[]{:S(2)}) copy-start(bf16[128,3072]{1,0:T(8,128)(2,1)} %param.15) | copy-start | bytes 2359300
  356.8 10.3 %copy-start.18 = (s32[128]{0:T(128)S(1)}, s32[128]{0:T(128)}, u32[]{:S(2)}) copy-start(s32[128]{0:T(128)} %copy-done.17) | copy-start | bytes 1540
  361.2 8.2 %copy-start.12 = (bf16[8,128,384]{2,1,0:T(8,128)(2,1)}, bf16[8,128,384]{2,1,0:T(8,128)(2,1)S(1)}, u32[]{:S(2)}) copy-start(bf16[8,128,384]{2,1,0:T(8,128)(2,1)S(1)} %all-to-all-done.5) | copy-start | bytes 2359300
  361.2 16.9 %all-to-all-start.6 = ((bf16[8,128,384]{2,1,0:T(8,128)(2,1)}), bf16[8,128,384]{2,1,0:T(8,128)(2,1)}, u32[]{:S(2)}, u32[]{:S(2)}) async-start(bf16[8,128,384]{2,1,0:T(8,128)(2,1)} %bitcast.18), calls=%async_computation.6 | async-start | bytes 1572864 | tf_op jit(solution)/shard_map/all_to_all | solution.py:167
  366.8 294.8 %all-reduce.2.cloned.1.call-start = ((), (), s32[]{:S(2)}) async-start(), calls=%async_computation.8 | async-start | bytes 3145728 | tf_op jit(solution)/shard_map/psum | solution.py:173
  369.4 14.8 %copy-start.10 = (f32[128,3072]{1,0:T(8,128)S(1)}, f32[128,3072]{1,0:T(8,128)}, u32[]{:S(2)}) copy-start(f32[128,3072]{1,0:T(8,128)} %get-tuple-element.232) | copy-start | bytes 4718596
  378.1 17.4 %all-to-all-start.7 = ((bf16[8,128,384]{2,1,0:T(8,128)(2,1)}), bf16[8,128,384]{2,1,0:T(8,128)(2,1)}, u32[]{:S(2)}, u32[]{:S(2)}) async-start(bf16[8,128,384]{2,1,0:T(8,128)(2,1)} %bitcast.137), calls=%async_computation.7 | async-start | bytes 1572864 | tf_op jit(solution)/shard_map/all_to_all | solution.py:168
  386.8 277.5 %copy-start.1 = (f32[128,3072]{1,0:T(8,128)S(1)}, f32[128,3072]{1,0:T(8,128)}, u32[]{:S(2)}) copy-start(f32[128,3072]{1,0:T(8,128)} %param.16) | copy-start | bytes 4718596
Sparse Core Ops, SparseCore 0:
  373.0 288.5 all-reduce.1
where the time goes:
time: 675 us; the launch traced here: 671 us
  waiting for transfers between devices  358 us (53%)
  local copies, waits for them, and re-layouts  141 us (21%)
  matrix products  68 us (10%)
  starting transfers between devices  56.4 us (8%)
  other arithmetic  28.3 us (4%)
  between operations  14.3 us (2%)
    psum x1, waiting for transfers between devices, per_device(): gate_grad = lax.psum(gate_part, ('ctx', 'head'))  263 us
    dynamic_update_slice x2, local copies, waits for them, and re-layouts, one_block(): partials = lax.dynamic_update_slice_in_dim(partials, window_part, offset, 1)  50.1 us
    all_to_all x1, waiting for transfers between devices, per_device(): lax.all_to_all(queries, 'head', split_axis=1, concat_axis=0, tiled=True)  32.9 us
    all_to_all x1, waiting for transfers between devices, per_device(): lax.all_to_all(attended, 'head', split_axis=0, concat_axis=1, tiled=True)  25.7 us
    dot_general x2, matrix products, attend(): jnp.einsum('hqk,khd->qhd', attention_low, v_heads, preferred_element_type...  17.2 us
    while x40, local copies, waits for them, and re-layouts  15.6 us
    unnamed x33, local copies, waits for them, and re-layouts  13.8 us
  transfers between devices with their start and end apart: 13, of which 9 were waited for; matrix products, arithmetic and copies ran while one was open for 8% of the time, Pallas kernels for 0%

commit v1 on v0

v1 whole, which is shorter than its diff:
```python
import functools
import math

import jax
import jax.numpy as jnp
from jax import lax
from jax.experimental import pallas as pl
from jax.experimental.pallas import tpu as pltpu
from jax.sharding import PartitionSpec as P

DH = 128
SPAN = 256
WINDOW = 1024
TILE = 256
SLAB = WINDOW + TILE + SPAN
BUF = 2 * WINDOW + SPAN
SCALE = 1.0 / math.sqrt(DH)
LOG2E = 1.0 / math.log(2.0)
HIDDEN = -1e30
F32 = jnp.float32
BF16 = jnp.bfloat16


def mm(a, b, contract=((1,), (0,))):
    return lax.dot_general(a, b, (contract, ((), ())), preferred_element_type=F32)


def prepare(span_ref, noise_ref, mask_ref, tab_ref, spans_k, bias, gate, level_t):
    spans = mask_ref.shape[0]
    levels = tab_ref.shape[1]
    row = lax.broadcasted_iota(jnp.int32, (spans, BUF), 0)
    onehot_t = (span_ref[...] == row).astype(F32)
    spans_k[...] = onehot_t.T.astype(BF16)
    own = onehot_t[:, WINDOW : 2 * WINDOW].astype(BF16)
    qs = lax.broadcasted_iota(jnp.int32, (spans, spans), 0)
    ks = lax.broadcasted_iota(jnp.int32, (spans, spans), 1)
    allowed = jnp.where(ks <= qs, mask_ref[...], 0).astype(F32).T.astype(BF16)
    mask_t = mm(allowed, own).astype(BF16)
    for t in range(WINDOW // TILE):
        seen = mm(spans_k[t * TILE : t * TILE + SLAB, :], mask_t[:, t * TILE : (t + 1) * TILE])
        bias[t] = jnp.where(seen > 0.5, 0.0, HIDDEN)
        k_pos = lax.broadcasted_iota(jnp.int32, (TILE, TILE), 0)
        q_pos = lax.broadcasted_iota(jnp.int32, (TILE, TILE), 1)
        bias[t, 0:TILE, :] = jnp.where(k_pos > q_pos, bias[t, 0:TILE, :], HIDDEN)
    lev = lax.broadcasted_iota(jnp.int32, (levels, spans), 0)
    span_level = (noise_ref[...] == lev).astype(BF16)
    level_t[...] = mm(span_level, own).astype(BF16)
    level = mm(spans_k[WINDOW : 2 * WINDOW, :], span_level, ((1,), (1,))).astype(BF16)
    for h in range(tab_ref.shape[0]):
        table = tab_ref[h]
        high = table.astype(BF16)
        low = (table - high.astype(F32)).astype(BF16)
        gate[h] = mm(level, high) + mm(level, low)


def attend_head(h, kv, qg, bias, gate, level_t, acc, res, gate_part):
    acc[...] = jnp.zeros_like(acc)

    def tile(t, level_sum):
        q_at = pl.ds(pl.multiple_of(t * TILE, TILE), TILE)
        k_at = pl.ds(pl.multiple_of(t * TILE, TILE), SLAB)
        k = kv[h, 0, k_at, :]
        v = kv[h, 1, k_at, :]
        q = qg[h, 0, q_at, :]
        cot = qg[h, 1, q_at, :].astype(F32)
        gate_rows = gate[h, q_at, :]
        g = (gate_rows * cot).astype(BF16)
        g_t = g.astype(F32).T
        z = mm(k, q, ((1,), (1,))) * (SCALE * LOG2E) + bias[t]
        top = jnp.max(z, axis=0, keepdims=True)
        e = jnp.exp2(z - top)
        inv = 1.0 / jnp.sum(e, axis=0, keepdims=True)
        e_low = e.astype(BF16)
        att_t = (mm(v, e_low, ((0,), (0,))) * inv).astype(BF16).astype(F32)
        dot = jnp.sum(g_t * att_t, axis=0, keepdims=True) * inv
        gs_t = (g_t * inv).astype(BF16)
        att = att_t.T
        d_prob = mm(v, gs_t)
        ds = (e * (d_prob - dot)).astype(BF16)
        acc[1, k_at, :] += mm(e_low, gs_t, ((1,), (1,)))
        acc[0, k_at, :] += mm(ds, q)
        dq_t = mm(k, ds, ((0,), (0,))) * SCALE
        res[h, 0, q_at, :] = (gate_rows * att).astype(BF16)
        res[h, 1, q_at, :] = dq_t.T.astype(BF16)
        prod = cot * att
        high = prod.astype(BF16)
        low = (prod - high.astype(F32)).astype(BF16)
        lev = level_t[:, q_at]
        return level_sum + mm(lev, high) + mm(lev, low)

    zero = jnp.zeros((level_t.shape[0], DH), F32)
    gate_part[h] = lax.fori_loop(0, WINDOW // TILE, tile, zero)


def kernel(span_ref, noise_ref, mask_ref, tab_ref, kv, qg, res, own, behind, ahead, gate_part,
           spans_k, bias, gate, level_t, acc):
    prepare(span_ref, noise_ref, mask_ref, tab_ref, spans_k, bias, gate, level_t)
    for h in range(kv.shape[0]):
        attend_head(h, kv, qg, bias, gate, level_t, acc, res, gate_part)
        for i, s in ((0, SCALE), (1, 1.0)):
            behind[h, i] = (acc[i, 0:WINDOW, :] * s).astype(BF16)
            own[h, i] = acc[i, WINDOW : 2 * WINDOW, :] * s
            ahead[h, i] = (acc[i, 2 * WINDOW :, :] * s).astype(BF16)


def attention(spans, noise, mask, tab, kv, qg):
    heads = kv.shape[0]
    vmem = pl.BlockSpec(memory_space=pltpu.VMEM)
    span_total = mask.shape[0]
    levels = tab.shape[1]
    return pl.pallas_call(
        kernel,
        out_shape=[
            jax.ShapeDtypeStruct((heads, 2, WINDOW, DH), BF16),
            jax.ShapeDtypeStruct((heads, 2, WINDOW, DH), F32),
            jax.ShapeDtypeStruct((heads, 2, WINDOW, DH), BF16),
            jax.ShapeDtypeStruct((heads, 2, SPAN, DH), BF16),
            jax.ShapeDtypeStruct((heads, levels, DH), F32),
        ],
        in_specs=[vmem] * 6,
        out_specs=[vmem] * 5,
        scratch_shapes=[
            pltpu.VMEM((BUF, span_total), BF16),
            pltpu.VMEM((WINDOW // TILE, SLAB, TILE), F32),
            pltpu.VMEM((heads, WINDOW, DH), F32),
            pltpu.VMEM((levels, WINDOW), BF16),
            pltpu.VMEM((2, BUF, DH), F32),
        ],
        compiler_params=pltpu.CompilerParams(vmem_limit_bytes=56 * 1024 * 1024),
    )(spans, noise, mask, tab, kv, qg)


def shifted(x, by):
    n = lax.axis_size("ctx")
    return lax.ppermute(x, "ctx", [(i, (i + by) % n) for i in range(n)])


def per_device(queries, key_rows, value_rows, out_cotangent, gate_table, span_ids, noise_level, block_mask):
    groups = lax.axis_size("head")
    rows, width = queries.shape
    heads = width // groups // DH
    ctx = lax.axis_index("ctx")
    head = lax.axis_index("head")
    padded = jnp.pad(span_ids, (WINDOW, SPAN), constant_values=-1)
    spans = lax.dynamic_slice_in_dim(padded, ctx * WINDOW, BUF, 0)[None, :]
    tab = lax.dynamic_slice_in_dim(gate_table, head * heads * DH, heads * DH, 1)
    tab = tab.reshape(-1, heads, DH).transpose(1, 0, 2)

    def to_heads(*arrays):
        x = jnp.stack(arrays).reshape(len(arrays), rows, groups, heads, DH).transpose(2, 3, 0, 1, 4)
        x = lax.all_to_all(x, "head", 0, 0, tiled=True)
        return x.transpose(1, 2, 0, 3, 4).reshape(heads, len(arrays), WINDOW, DH)

    def to_tokens(x):
        x = x.reshape(heads, 2, groups, rows, DH).transpose(2, 0, 1, 3, 4)
        x = lax.all_to_all(x, "head", 0, 0, tiled=True)
        x = x.transpose(2, 3, 0, 1, 4).reshape(2, rows, width)
        return x[0], x[1]

    kv_own = to_heads(key_rows, value_rows)
    qg = to_heads(queries, out_cotangent)
    kv = jnp.concatenate([shifted(kv_own, 1), kv_own, shifted(kv_own[:, :, :SPAN], -1)], axis=2)
    res, own, behind, ahead, gate_part = attention(
        spans, noise_level[None, :], block_mask, tab, kv, qg
    )
    own = own + shifted(behind, -1).astype(F32)
    own = own.at[:, :, :SPAN].add(shifted(ahead, 1).astype(F32))
    gate_sum = lax.psum(gate_part, "ctx")
    gate_grad = lax.all_gather(gate_sum, "head", axis=0, tiled=True)
    gate_grad = gate_grad.transpose(1, 0, 2).reshape(-1, width)
    mixed_out, query_grad = to_tokens(res)
    key_grad, value_grad = to_tokens(own.astype(BF16))
    return mixed_out, query_grad, key_grad, value_grad, gate_grad


def solution(mesh):
    split = P(("ctx", "head"), None)
    return jax.shard_map(
        per_device,
        mesh=mesh,
        in_specs=(split, split, split, split, P(), P(), P(), P()),
        out_specs=(split, split, split, split, P()),
        check_vma=False,
    )
```

time: 675 us -> 422 us (0.63)
  local copies, waits for them, and re-layouts: 141 us -> 31.4 us
  waiting for transfers between devices: 358 us -> 283 us
  matrix products: 68 us -> 0 us
  starting transfers between devices: 56.4 us -> 22.4 us
  Pallas kernels: 0 us -> 32.5 us
  blocking collectives: 0 us -> 28.6 us
  other arithmetic: 28.3 us -> 9.12 us
    dot_general x16 -> x0, matrix products: 68 us -> none  [the longest x2 17.2 us: attend(): jnp.einsum('hqk,khd->qhd', attention_low, v_heads, preferred_element_type...]
    all_to_all x8 -> x3, waiting for transfers between devices: 93.3 us -> 25.5 us  [the longest x1 25.5 us: to_heads(): x = lax.all_to_all(x, 'head', 0, 0, tiled=True)]
    dynamic_update_slice x8 -> x0, local copies, waits for them, and re-layouts: 54.9 us -> none  [the longest x2 50.1 us: one_block(): partials = lax.dynamic_update_slice_in_dim(partials, window_part, offset, 1)]
    psum x1, waiting for transfers between devices: 263 us -> 209 us  [per_device(): gate_sum = lax.psum(gate_part, 'ctx')]
    pallas_call x0 -> x1, Pallas kernels: none -> 32.5 us  [attention(): pl.pallas_call(kernel, out_shape=[jax.ShapeDtypeStruct((heads, 2, WINDOW,...]
    all_gather x0 -> x1, waiting for transfers between devices: none -> 29.2 us  [per_device(): gate_grad = lax.all_gather(gate_sum, 'head', axis=0, tiled=True)]
    all_to_all x0 -> x1, blocking collectives: none -> 28.6 us  [to_heads(): x = lax.all_to_all(x, 'head', 0, 0, tiled=True)]
    all_to_all x8 -> x3, starting transfers between devices: 43.7 us -> 17.3 us  [the longest x2 12.9 us: to_tokens(): x = lax.all_to_all(x, 'head', 0, 0, tiled=True)]
  transfers between devices with their start and end apart: 13 -> 9, of which waited for: 9 -> 4; matrix products, arithmetic and copies ran while one was open for 8% -> 7% of each run, Pallas kernels for 0% -> 0%
where the time goes in v1:
time: 422 us; the launch traced here: 421 us
  waiting for transfers between devices  283 us (67%)
  Pallas kernels  32.5 us (8%)
  local copies, waits for them, and re-layouts  31.4 us (7%)
  blocking collectives  28.6 us (7%)
  starting transfers between devices  22.4 us (5%)
  between operations  14.2 us (3%)
  other arithmetic  9.12 us (2%)
    psum x1, waiting for transfers between devices, per_device(): gate_sum = lax.psum(gate_part, 'ctx')  209 us
    pallas_call x1, Pallas kernels, attention(): pl.pallas_call(kernel, out_shape=[jax.ShapeDtypeStruct((heads, 2, WINDOW,...  32.5 us
    all_gather x1, waiting for transfers between devices, per_device(): gate_grad = lax.all_gather(gate_sum, 'head', axis=0, tiled=True)  29.2 us
    all_to_all x1, blocking collectives, to_heads(): x = lax.all_to_all(x, 'head', 0, 0, tiled=True)  28.6 us
    all_to_all x1, waiting for transfers between devices, to_heads(): x = lax.all_to_all(x, 'head', 0, 0, tiled=True)  25.5 us
    ppermute x4, waiting for transfers between devices, shifted(): return lax.ppermute(x, 'ctx', [(i, (i + by) % n) for i in range(n)])  19.3 us
    unnamed x16, local copies, waits for them, and re-layouts  14.1 us
    all_to_all x2, starting transfers between devices, to_tokens(): x = lax.all_to_all(x, 'head', 0, 0, tiled=True)  12.9 us
  transfers between devices with their start and end apart: 9, of which 4 were waited for; matrix products, arithmetic and copies ran while one was open for 7% of the time, Pallas kernels for 0%

profile of v1, /device:TPU:1, one launch (start us, length us, event | category | flops | bytes accessed | tf_op | source)
XLA Modules:
  0.0 421.2 jit_solution(10056052670484927664)
XLA Ops:
  7.2 0.0 copy-start
  7.2 1.6 copy.39
  8.8 1.5 copy.40
  10.3 0.1 maximum_bitcast_fusion
  10.5 0.2 copy.41
  10.7 28.6 %all_to_all.20 = bf16[8,3,2,128,128]{3,4,1,2,0:T(8,128)(2,1)} all-to-all(bf16[8,3,2,128,128]{3,4,1,2,0:T(8,128)(2,1)S(1)} %copy.41), channel_id=1, replica_groups=mesh['ctx'=32,'head'=8] {'head'}, dimensions={0} | all-to-all | bytes 3145728 | tf_op jit(solution)/shard_map/all_to_all | solution.py:151
  39.2 1.9 copy.42
  41.2 3.0 collective-permute-start
  44.1 2.3 copy.43
  46.4 2.3 copy.44
  48.7 1.5 maximum_bitcast_fusion.1
  50.2 1.2 copy.45
  51.5 4.4 %all-to-all-start.1 = ((bf16[8,3,2,128,128]{3,4,1,2,0:T(8,128)(2,1)}), bf16[8,3,2,128,128]{3,4,1,2,0:T(8,128)(2,1)}, u32[]{:S(2)}, u32[]{:S(2)}) async-start(bf16[8,3,2,128,128]{3,4,1,2,0:T(8,128)(2,1)} %copy.45), calls=%async_computation.1 | async-start | bytes 3145728 | tf_op jit(solution)/shard_map/all_to_all | solution.py:151
  55.9 0.0 all-reduce.3.cloned.1.call-start
  55.9 0.8 slice.54
  56.7 0.1 pad_dynamic-slice_fusion
  56.8 0.6 broadcast_in_dim.6.span_ref
  57.4 0.1 copy.57
  57.6 0.8 copy.38
  58.4 25.5 %all-to-all-done.1 = bf16[8,3,2,128,128]{3,4,1,2,0:T(8,128)(2,1)} async-done(((bf16[8,3,2,128,128]{3,4,1,2,0:T(8,128)(2,1)}), bf16[8,3,2,128,128]{3,4,1,2,0:T(8,128)(2,1)}, u32[]{:S(2)}, u32[]{:S(2)}) %all-to-all-start.1) | async-done | bytes 1572896 | tf_op jit(solution)/shard_map/all_to_all | solution.py:151
  83.9 2.6 copy.46
  86.5 3.3 pad_maximum_fusion.kv
  89.8 32.5 %shard_map.119 = (bf16[3,2,1024,128]{3,2,1,0:T(8,128)(2,1)}, f32[3,2,1024,128]{3,2,1,0:T(8,128)}, bf16[3,2,1024,128]{3,2,1,0:T(8,128)(2,1)}, bf16[3,2,256,128]{3,2,1,0:T(8,128)(2,1)}, f32[3,128,128]{2,1,0:T(8,128)}) custom-call(s32[1,2304]{1,0:T(1,128)} %broadcast_in_dim.6.span_ref, s32[1,192]{1,0:T(1,128)} %bitcast.53, s32[192,192]{1,0:T(8,128)} %mask_ref.1, ...), custom_call_target="tpu_custom_call" | custom-call | tf_op jit(solution)/shard_map/pallas_call | solution.py:111
  122.3 0.0 all-reduce.3.cloned.1.call-update
  122.3 0.0 all-gather.2.cloned.1.call-start
  122.4 2.6 copy.47
  124.9 209.1 %all-reduce.3.cloned.1.call-done = f32[3,128,128]{2,1,0:T(8,128)} async-done(((f32[3,128,128]{2,1,0:T(8,128)}), f32[3,128,128]{2,1,0:T(8,128)}) %all-reduce.3.cloned.1.call-update) | async-done | bytes 196624 | tf_op jit(solution)/shard_map/psum | solution.py:168
  334.0 0.0 all-gather.2.cloned.1.call-update
  334.1 0.0 copy-start.2
  334.1 6.3 %all-to-all-start.2 = ((bf16[8,3,2,128,128]{3,4,1,2,0:T(8,128)(2,1)}), bf16[8,3,2,128,128]{3,4,1,2,0:T(8,128)(2,1)S(1)}, u32[]{:S(2)}, u32[]{:S(2)}) async-start(bf16[8,3,2,128,128]{3,4,1,2,0:T(8,128)(2,1)} %bitcast.14), calls=%async_computation.2 | async-start | bytes 3145728 | tf_op jit(solution)/shard_map/all_to_all | solution.py:156
  340.3 2.0 collective-permute-start.3
  342.3 2.6 convert_add_fusion
  344.9 19.3 %collective-permute-done.3 = bf16[3,2,256,128]{3,2,1,0:T(8,128)(2,1)S(1)} collective-permute-done((bf16[3,2,256,128]{3,2,1,0:T(8,128)(2,1)S(1)}, bf16[3,2,256,128]{3,2,1,0:T(8,128)(2,1)S(1)}, u32[]{:S(2)}, u32[]{:S(2)}) %collective-permute-start.3) | collective-permute-done | bytes 393248 | tf_op jit(solution)/shard_map/ppermute | solution.py:135
  364.2 0.2 fusion
  364.4 1.4 convert_element_type.11
  365.8 2.6 copy.49
  368.4 6.6 %all-to-all-start.3 = ((bf16[8,3,2,128,128]{3,4,1,2,0:T(8,128)(2,1)}), bf16[8,3,2,128,128]{3,4,1,2,0:T(8,128)(2,1)}, u32[]{:S(2)}, u32[]{:S(2)}) async-start(bf16[8,3,2,128,128]{3,4,1,2,0:T(8,128)(2,1)} %bitcast.35), calls=%async_computation.3 | async-start | bytes 3145728 | tf_op jit(solution)/shard_map/all_to_all | solution.py:156
  375.0 0.2 copy.61
  375.2 0.2 fusion.2
  375.4 1.2 copy.53
  376.5 1.2 copy.52
  377.7 29.2 %all-gather.2.cloned.1.call-done = f32[24,128,128]{2,1,0:T(8,128)} async-done(((f32[3,128,128]{2,1,0:T(8,128)}), f32[24,128,128]{2,1,0:T(8,128)}) %all-gather.2.cloned.1.call-update) | async-done | bytes 1572880 | tf_op jit(solution)/shard_map/all_gather | solution.py:169
  406.9 1.9 copy.51
  408.7 1.6 copy.56
  410.3 1.5 copy.60
  411.9 0.2 fusion.1
  412.0 1.2 copy.55
  413.2 1.2 copy.54
  (12 shorter events, 0.0 us)
Async XLA Ops:
  7.2 50.3 %copy-start = (f32[128,3072]{1,0:T(8,128)S(1)}, f32[128,3072]{1,0:T(8,128)}, u32[]{:S(2)}) copy-start(f32[128,3072]{1,0:T(8,128)} %param.14) | copy-start | bytes 4718596
  41.2 45.3 %collective-permute-start = (bf16[3,2,1024,128]{3,2,1,0:T(8,128)(2,1)S(1)}, bf16[3,2,1024,128]{3,2,1,0:T(8,128)(2,1)}, u32[]{:S(2)}, u32[]{:S(2)}) collective-permute-start(bf16[3,2,1024,128]{3,2,1,0:T(8,128)(2,1)S(1)} %bitcast.32), channel_id=1, source_target_pairs={{0,8},{8,16},{16,24},{24,32},{32,40},{40,48},{48,56},{56,64},{64,7... | collective-permute-start | bytes 4718600 | tf_op jit(solution)/shard_map/ppermute | solution.py:135
  51.5 5.3 %copy-start.1 = (s32[32768]{0:T(1024)S(1)}, s32[32768]{0:T(1024)}, u32[]{:S(2)}) copy-start(s32[32768]{0:T(1024)} %param.15) | copy-start | bytes 393220
  51.5 32.4 %all-to-all-start.1 = ((bf16[8,3,2,128,128]{3,4,1,2,0:T(8,128)(2,1)}), bf16[8,3,2,128,128]{3,4,1,2,0:T(8,128)(2,1)}, u32[]{:S(2)}, u32[]{:S(2)}) async-start(bf16[8,3,2,128,128]{3,4,1,2,0:T(8,128)(2,1)} %copy.45), calls=%async_computation.1 | async-start | bytes 3145728 | tf_op jit(solution)/shard_map/all_to_all | solution.py:151
  55.9 278.1 %all-reduce.3.cloned.1.call-start = ((), (), s32[]{:S(2)}) async-start(), calls=%async_computation.4 | async-start | bytes 393216 | tf_op jit(solution)/shard_map/psum | solution.py:168
  56.7 29.7 %collective-permute-start.1 = (bf16[3,2,256,128]{3,2,1,0:T(8,128)(2,1)}, bf16[3,2,256,128]{3,2,1,0:T(8,128)(2,1)}, u32[]{:S(2)}, u32[]{:S(2)}) collective-permute-start(bf16[3,2,256,128]{3,2,1,0:T(8,128)(2,1)} %slice.54), channel_id=1, source_target_pairs={{0,248},{8,0},{16,8},{24,16},{32,24},{40,32},{48,40},{56,48},{64,5... | collective-permute-start | bytes 1179656 | tf_op jit(solution)/shard_map/ppermute | solution.py:135
  122.3 220.0 %collective-permute-start.2 = (bf16[3,2,1024,128]{3,2,1,0:T(8,128)(2,1)}, bf16[3,2,1024,128]{3,2,1,0:T(8,128)(2,1)}, u32[]{:S(2)}, u32[]{:S(2)}) collective-permute-start(bf16[3,2,1024,128]{3,2,1,0:T(8,128)(2,1)} %get-tuple-element.24), channel_id=1, source_target_pairs={{0,248},{8,0},{16,8},{24,16},{32,24},{40,32},{48,40},{56,48},{64,5... | collective-permute-start | bytes 4718600 | tf_op jit(solution)/shard_map/ppermute | solution.py:135
  122.3 284.5 %all-gather.2.cloned.1.call-start = ((), (), s32[]{:S(2)}) async-start(), calls=%async_computation.5 | async-start | bytes 1769472 | tf_op jit(solution)/shard_map/all_gather | solution.py:169
  334.1 6.3 %copy-start.2 = (bf16[3,2,256,128]{3,2,1,0:T(8,128)(2,1)S(1)}, bf16[3,2,256,128]{3,2,1,0:T(8,128)(2,1)}, u32[]{:S(2)}) copy-start(bf16[3,2,256,128]{3,2,1,0:T(8,128)(2,1)} %get-tuple-element.25) | copy-start | bytes 1179652
  334.1 34.3 %all-to-all-start.2 = ((bf16[8,3,2,128,128]{3,4,1,2,0:T(8,128)(2,1)}), bf16[8,3,2,128,128]{3,4,1,2,0:T(8,128)(2,1)S(1)}, u32[]{:S(2)}, u32[]{:S(2)}) async-start(bf16[8,3,2,128,128]{3,4,1,2,0:T(8,128)(2,1)} %bitcast.14), calls=%async_computation.2 | async-start | bytes 3145728 | tf_op jit(solution)/shard_map/all_to_all | solution.py:156
  340.3 23.9 %collective-permute-start.3 = (bf16[3,2,256,128]{3,2,1,0:T(8,128)(2,1)S(1)}, bf16[3,2,256,128]{3,2,1,0:T(8,128)(2,1)S(1)}, u32[]{:S(2)}, u32[]{:S(2)}) collective-permute-start(bf16[3,2,256,128]{3,2,1,0:T(8,128)(2,1)S(1)} %copy-done.2), channel_id=1, source_target_pairs={{0,8},{8,16},{16,24},{24,32},{32,40},{40,48},{48,56},{56,64},{64,7... | collective-permute-start | bytes 1179656 | tf_op jit(solution)/shard_map/ppermute | solution.py:135
  368.4 42.0 %all-to-all-start.3 = ((bf16[8,3,2,128,128]{3,4,1,2,0:T(8,128)(2,1)}), bf16[8,3,2,128,128]{3,4,1,2,0:T(8,128)(2,1)}, u32[]{:S(2)}, u32[]{:S(2)}) async-start(bf16[8,3,2,128,128]{3,4,1,2,0:T(8,128)(2,1)} %bitcast.35), calls=%async_computation.3 | async-start | bytes 3145728 | tf_op jit(solution)/shard_map/all_to_all | solution.py:156
Sparse Core Ops, SparseCore 0:
  122.4 211.5 all-reduce.2
  337.0 69.8 all-gather.1

commit v2 on v1

v2 whole, which is shorter than its diff:
```python
import functools
import math

import jax
import jax.numpy as jnp
from jax import lax
from jax.experimental import pallas as pl
from jax.experimental.pallas import tpu as pltpu
from jax.sharding import PartitionSpec as P

DH = 128
SPAN = 256
WINDOW = 1024
TILE = 256
BLOCK = 128
SLAB = WINDOW + TILE + SPAN
QA = 2 * WINDOW
QB = WINDOW
PLANE = 4 * WINDOW
SCALE = 1.0 / math.sqrt(DH)
LOG2E = 1.0 / math.log(2.0)
HIDDEN = -1e30
F32 = jnp.float32
BF16 = jnp.bfloat16
MESH = pl.DeviceIdType.MESH


def mm(a, b, contract=((1,), (0,))):
    return lax.dot_general(a, b, (contract, ((), ())), preferred_element_type=F32)


def place(z, x, y, core):
    return (z * 4 + lax.rem(x, 2) * 2 + core, lax.div(x, 2) * 4 + y)


def where_am_i():
    ctx = lax.axis_index("ctx")
    head = lax.axis_index("head")
    z = lax.div(ctx, 4)
    x = lax.div(head, 4) * 2 + lax.rem(lax.div(ctx, 2), 2)
    return z, x, lax.rem(head, 4), lax.rem(ctx, 2)


def whole_head(x, y):
    return x * 4 + y


def shared_head(x, y):
    return 16 + lax.div(x, 2) * 4 + y


def prepare(span_ref, noise_ref, mask_ref, tab_ref, spans_k, bias, gate, level_t):
    spans = mask_ref.shape[0]
    levels = tab_ref.shape[0]
    queries = bias.shape[0] * TILE
    rows = queries + WINDOW + SPAN
    row = lax.broadcasted_iota(jnp.int32, (spans, rows), 0)
    onehot_t = (span_ref[...] == row).astype(F32)
    spans_k[0:rows, :] = onehot_t.T.astype(BF16)
    own = onehot_t[:, WINDOW : WINDOW + queries].astype(BF16)
    qs = lax.broadcasted_iota(jnp.int32, (spans, spans), 0)
    ks = lax.broadcasted_iota(jnp.int32, (spans, spans), 1)
    allowed = jnp.where(ks <= qs, mask_ref[...], 0).astype(F32).T.astype(BF16)
    mask_t = mm(allowed, own).astype(BF16)
    k_pos = lax.broadcasted_iota(jnp.int32, (TILE, TILE), 0)
    q_pos = lax.broadcasted_iota(jnp.int32, (TILE, TILE), 1)
    for t in range(bias.shape[0]):
        seen = mm(spans_k[t * TILE : t * TILE + SLAB, :], mask_t[:, t * TILE : (t + 1) * TILE])
        shown = jnp.where(seen > 0.5, 0.0, HIDDEN)
        bias[t, TILE:, :] = shown[TILE:, :]
        bias[t, 0:TILE, :] = jnp.where(k_pos > q_pos, shown[0:TILE, :], HIDDEN)
    lev = lax.broadcasted_iota(jnp.int32, (levels, spans), 0)
    span_level = (noise_ref[...] == lev).astype(BF16)
    level_t[...] = mm(span_level, own).astype(BF16)
    level = mm(spans_k[WINDOW : WINDOW + queries, :], span_level, ((1,), (1,))).astype(BF16)
    table = tab_ref[...]
    high = table.astype(BF16)
    low = (table - high.astype(F32)).astype(BF16)
    gate[...] = mm(level, high) + mm(level, low)


def attend_tile(t, kv, qg, bias, gate, level_t, acc, res, level_sum):
    q_at = pl.ds(pl.multiple_of(t * TILE, TILE), TILE)
    k_at = pl.ds(pl.multiple_of(t * TILE, TILE), SLAB)
    k = kv[0, k_at, :]
    v = kv[1, k_at, :]
    q = qg[0, q_at, :]
    cot = qg[1, q_at, :].astype(F32)
    gate_rows = gate[q_at, :]
    g_t = (gate_rows * cot).astype(BF16).astype(F32).T
    z = mm(k, q, ((1,), (1,))) * (SCALE * LOG2E) + bias[t]
    top = jnp.max(z, axis=0, keepdims=True)
    e = jnp.exp2(z - top)
    inv = 1.0 / jnp.sum(e, axis=0, keepdims=True)
    e_low = e.astype(BF16)
    att_t = (mm(v, e_low, ((0,), (0,))) * inv).astype(BF16).astype(F32)
    dot = jnp.sum(g_t * att_t, axis=0, keepdims=True) * inv
    gs_t = (g_t * inv).astype(BF16)
    att = att_t.T
    d_prob = mm(v, gs_t)
    ds = (e * (d_prob - dot)).astype(BF16)
    acc[1, k_at, :] += mm(e_low, gs_t, ((1,), (1,)))
    acc[0, k_at, :] += mm(ds, q)
    dq_t = mm(k, ds, ((0,), (0,))) * SCALE
    res[0, q_at, :] = (gate_rows * att).astype(BF16)
    res[1, q_at, :] = dq_t.T.astype(BF16)
    prod = cot * att
    high = prod.astype(BF16)
    low = (prod - high.astype(F32)).astype(BF16)
    lev = level_t[:, q_at]
    level_sum[...] += mm(lev, high) + mm(lev, low)


def kernel(
    nz, span_a, span_b, noise_ref, mask_ref, tab_a, tab_b, q_ref, k_ref, v_ref, c_ref,
    out_mq, out_kv, out_gate,
    st_kv, st_qg, kv_a, kv_b, qg_a, qg_b, spans_k, bias_a, bias_b, gate_a, gate_b, lev_a, lev_b,
    acc_a, acc_b, res_a, res_b, dkv_a, dkv_b, sb_a, sb_b, sa_a, sa_b, rb_a, rb_b, ra_a, ra_b,
    gate_part, gate_pair, gate_all, pieces, sums, full, full_low, gate_buf,
    load_sem, in_send, in_recv, halo_send, halo_recv, part_send, part_recv, out_send, out_recv,
    gate_send, gate_recv,
):
    z, x, y, core = where_am_i()
    x_lo = lax.rem(x, 2)
    own_block = lax.div(x, 2) * 4 + y
    stays = core == x_lo
    pair_x = x + 1 - 2 * x_lo
    group = 2 * nz
    member = z * 2 + core
    piece = sums.shape[1]

    def remote(src, dst, send, recv, to):
        return pltpu.make_async_remote_copy(
            src_ref=src, dst_ref=dst, send_sem=send, recv_sem=recv, device_id=to, device_id_type=MESH
        )

    def took(ref, sem):
        pltpu.make_async_copy(ref, ref, sem).wait()

    def cols(head):
        return pl.ds(pl.multiple_of(head * DH, DH), DH)

    def rows(start, size):
        return pl.ds(pl.multiple_of(start, BLOCK), size)

    loads = [
        pltpu.make_async_copy(src, st.at[i], load_sem.at[n])
        for n, (src, st, i) in enumerate(
            ((k_ref, st_kv, 0), (v_ref, st_kv, 1), (q_ref, st_qg, 0), (c_ref, st_qg, 1))
        )
    ]
    for load in loads:
        load.start()

    barrier = pltpu.get_barrier_semaphore()
    spot = x * 8 + y * 2 + core

    def greet_plane(j, carry):
        other = lax.rem(spot + j, 32)
        to = place(z, lax.div(other, 8), lax.rem(lax.div(other, 2), 4), lax.rem(other, 2))
        pl.semaphore_signal(barrier, inc=1, device_id=to, device_id_type=MESH)
        return carry

    lax.fori_loop(1, 32, greet_plane, 0)

    def greet_column(j, carry):
        for c in range(2):
            to = place(lax.rem(z + j, nz), x, y, c)
            pl.semaphore_signal(barrier, inc=1, device_id=to, device_id_type=MESH)
        return carry

    lax.fori_loop(1, nz, greet_column, 0)
    for step in (1, nz - 1):
        to = place(lax.rem(z + step, nz), pair_x, y, 1 - core)
        pl.semaphore_signal(barrier, inc=1, device_id=to, device_id_type=MESH)
    pl.semaphore_wait(barrier, 31 + 2 * (nz - 1) + 2)

    def send_shared(st, dst, s):
        start = own_block * BLOCK
        at = dst.at[:, rows(WINDOW + start if dst is kv_b else start, BLOCK), :]
        for j in range(8):
            tx = lax.rem(x + 2 * (j % 2), 4)
            ty = lax.rem(y + j // 2, 4)
            src = st.at[:, :, cols(shared_head(tx, ty))]
            if j == 0:
                pltpu.make_async_copy(src, at, in_recv.at[s]).start()
            else:
                remote(src, at, in_send.at[s], in_recv.at[s], place(z, tx, ty, core)).start()

    def send_whole(st, dst, s):
        start = core * WINDOW + own_block * BLOCK
        at = dst.at[:, rows(WINDOW + start if dst is kv_a else start, BLOCK), :]
        for j in range(16):
            tx = lax.rem(x + j % 4, 4)
            ty = lax.rem(y + j // 4, 4)
            src = st.at[:, :, cols(whole_head(tx, ty))]
            go = remote(src, at, in_send.at[s], in_recv.at[s], place(z, tx, ty, x_lo))
            if j == 0:
                @pl.when(stays)
                def _():
                    pltpu.make_async_copy(src, at, in_recv.at[s]).start()

                @pl.when(jnp.logical_not(stays))
                def _():
                    go.start()
            else:
                go.start()

    loads[0].wait()
    loads[1].wait()
    send_shared(st_kv, kv_b, 0)
    loads[2].wait()
    loads[3].wait()
    send_shared(st_qg, qg_b, 1)
    send_whole(st_kv, kv_a, 2)

    prepare(span_b, noise_ref, mask_ref, tab_b, spans_k, bias_b, gate_b, lev_b)
    acc_b[...] = jnp.zeros_like(acc_b)
    gate_part[...] = jnp.zeros_like(gate_part)

    next_a = place(lax.rem(z + core, nz), x, y, 1 - core)
    prev_a = place(lax.rem(z + nz - 1 + core, nz), x, y, 1 - core)
    next_x = jnp.where(core == 0, x, pair_x)
    prev_x = jnp.where(core == 0, pair_x, x)
    next_b = place(lax.rem(z + core * x_lo, nz), next_x, y, 1 - core)
    prev_b = place(lax.rem(z + nz - (1 - core) * (1 - x_lo), nz), prev_x, y, 1 - core)

    def halo(kv, queries, n, after, before):
        last = WINDOW + queries
        return (
            remote(
                kv.at[:, queries:last, :], kv.at[:, 0:WINDOW, :], halo_send.at[n], halo_recv.at[n], after
            ),
            remote(
                kv.at[:, WINDOW : WINDOW + SPAN, :],
                kv.at[:, last : last + SPAN, :],
                halo_send.at[n + 1],
                halo_recv.at[n + 1],
                before,
            ),
        )

    halo_b = halo(kv_b, QB, 0, next_b, prev_b)
    halo_a = halo(kv_a, QA, 2, next_a, prev_a)

    took(kv_b.at[:, WINDOW : WINDOW + QB, :], in_recv.at[0])
    for c in halo_b:
        c.start()
    send_whole(st_qg, qg_a, 3)
    prepare(span_a, noise_ref, mask_ref, tab_a, spans_k, bias_a, gate_a, lev_a)
    acc_a[...] = jnp.zeros_like(acc_a)
    took(qg_b, in_recv.at[1])
    for c in halo_b:
        c.wait()

    def give_shared(buf, out, i, s):
        src = buf.at[:, rows(i * BLOCK, BLOCK), :]
        dst = out.at[:, :, cols(shared_head(x, y))]
        mine = i == own_block

        @pl.when(mine)
        def _():
            pltpu.make_async_copy(src, dst, out_recv.at[s]).start()

        @pl.when(jnp.logical_not(mine))
        def _():
            to = place(z, lax.div(i, 4) * 2 + x_lo, lax.rem(i, 4), core)
            remote(src, dst, out_send.at[s], out_recv.at[s], to).start()

    def give_whole(buf, out, i, s):
        src = buf.at[:, rows(i * BLOCK, BLOCK), :]
        dst = out.at[:, :, cols(whole_head(x, y))]
        mine = jnp.logical_and(stays, i == core * 8 + own_block)

        @pl.when(mine)
        def _():
            pltpu.make_async_copy(src, dst, out_recv.at[s]).start()

        @pl.when(jnp.logical_not(mine))
        def _():
            b = lax.rem(i, 8)
            to = place(z, lax.div(b, 4) * 2 + core, lax.rem(b, 4), lax.div(i, 8))
            remote(src, dst, out_send.at[2 + s], out_recv.at[s], to).start()

    def tile_b(t, carry):
        attend_tile(t, kv_b, qg_b, bias_b, gate_b, lev_b, acc_b, res_b, gate_part.at[1])
        for j in range(TILE // BLOCK):
            give_shared(res_b, out_mq, t * (TILE // BLOCK) + j, 0)
        return carry

    lax.fori_loop(0, QB // TILE, tile_b, 0)

    def part(buf, recv, n, to):
        return remote(buf, recv, part_send.at[n], part_recv.at[n], to)

    behind_b = part(sb_b, rb_b, 0, prev_b)
    ahead_b = part(sa_b, ra_b, 1, next_b)
    behind_a = part(sb_a, rb_a, 2, prev_a)
    ahead_a = part(sa_a, ra_a, 3, next_a)
    pair_gate = remote(
        gate_part.at[1], gate_pair, gate_send.at[0], gate_recv.at[0], place(z, pair_x, y, core)
    )

    for i, s in ((0, SCALE), (1, 1.0)):
        sb_b[i] = (acc_b[i, 0:WINDOW, :] * s).astype(BF16)
        sa_b[i] = (acc_b[i, WINDOW + QB :, :] * s).astype(BF16)
    behind_b.start()
    ahead_b.start()
    pair_gate.start()

    took(kv_a.at[:, WINDOW : WINDOW + QA, :], in_recv.at[2])
    for c in halo_a:
        c.start()
    took(qg_a, in_recv.at[3])
    for c in halo_a:
        c.wait()

    def finish_b():
        behind_b.wait()
        ahead_b.wait()
        for i, s in ((0, SCALE), (1, 1.0)):
            total = acc_b[i, WINDOW : WINDOW + QB, :] * s + rb_b[i].astype(F32)
            dkv_b[i] = total.astype(BF16)
            first = total[0:SPAN, :] + ra_b[i].astype(F32)
            dkv_b[i, 0:SPAN, :] = first.astype(BF16)

        def give(i, carry):
            give_shared(dkv_b, out_kv, i, 1)
            return carry

        lax.fori_loop(0, QB // BLOCK, give, 0)

    def tile_a(t, carry):
        attend_tile(t, kv_a, qg_a, bias_a, gate_a, lev_a, acc_a, res_a, gate_part.at[0])
        for j in range(TILE // BLOCK):
            give_whole(res_a, out_mq, t * (TILE // BLOCK) + j, 0)

        @pl.when(t == 1)
        def _():
            finish_b()

        @pl.when(t == 3)
        def _():
            for i, s in ((0, SCALE), (1, 1.0)):
                sb_a[i] = (acc_a[i, 0:WINDOW, :] * s).astype(BF16)
            behind_a.start()

        @pl.when(t >= 5)
        def _():
            own = pl.ds(pl.multiple_of((t - 4) * TILE, TILE), TILE)
            held = pl.ds(pl.multiple_of(t * TILE, TILE), TILE)
            dkv_a[0, own, :] = (acc_a[0, held, :] * SCALE).astype(BF16)
            dkv_a[1, own, :] = acc_a[1, held, :].astype(BF16)
            for j in range(TILE // BLOCK):
                give_whole(dkv_a, out_kv, (t - 4) * (TILE // BLOCK) + j, 1)

        return carry

    lax.fori_loop(0, QA // TILE, tile_a, 0)

    for i, s in ((0, SCALE), (1, 1.0)):
        sa_a[i] = (acc_a[i, WINDOW + QA :, :] * s).astype(BF16)
    ahead_a.start()

    pair_gate.wait()
    gate_all[0] = gate_part[0]
    gate_all[1] = gate_part[1] + gate_pair[...]
    at_mine = pl.ds(pl.multiple_of(member * piece, 8), piece)

    def to_member(j, carry):
        other = lax.rem(member + j, group)
        src = gate_all.at[:, pl.ds(pl.multiple_of(other * piece, 8), piece), :]
        to = place(lax.div(other, 2), x, y, lax.rem(other, 2))
        remote(src, pieces.at[member], gate_send.at[1], gate_recv.at[1], to).start()
        return carry

    lax.fori_loop(1, group, to_member, 0)

    def give_rest(i, carry):
        give_whole(dkv_a, out_kv, i, 1)
        return carry

    behind_a.wait()
    for i, s in ((0, SCALE), (1, 1.0)):
        total = acc_a[i, 2 * WINDOW : 2 * WINDOW + WINDOW, :] * s + rb_a[i].astype(F32)
        dkv_a[i, WINDOW:, :] = total.astype(BF16)
    lax.fori_loop(WINDOW // BLOCK, QA // BLOCK, give_rest, 0)

    took(pieces.at[0 : group - 1], gate_recv.at[1])
    total = gate_all[:, at_mine, :]
    for j in range(1, group):
        total = total + pieces[lax.rem(member + j, group)]
    sums[...] = total
    full[at_mine, :] = sums[core]

    def back_to_member(j, carry):
        other = lax.rem(member + j, group)
        c = lax.rem(other, 2)
        to = place(lax.div(other, 2), x, y, c)
        remote(sums.at[c], full.at[at_mine, :], gate_send.at[2], gate_recv.at[2], to).start()
        return carry

    lax.fori_loop(1, group, back_to_member, 0)

    ahead_a.wait()
    for i, s in ((0, SCALE), (1, 1.0)):
        first = acc_a[i, WINDOW : WINDOW + SPAN, :] * s + ra_a[i].astype(F32)
        dkv_a[i, 0:SPAN, :] = first.astype(BF16)
    lax.fori_loop(0, SPAN // BLOCK, give_rest, 0)

    took(full.at[0 : (group - 1) * piece, :], gate_recv.at[2])
    full_low[...] = full[...].astype(BF16)
    half = DH // 2
    at_half = pl.ds(pl.multiple_of(x_lo * half, half), half)
    other_core = place(z, x, y, 1 - core)
    split = whole_head(4, 0) * DH

    @pl.when(core == 0)
    def _():
        for j in range(1, 16):
            to = place(z, lax.rem(x + j % 4, 4), lax.rem(y + j // 4, 4), core)
            dst = gate_buf.at[:, cols(whole_head(x, y))]
            remote(full_low, dst, gate_send.at[3], gate_recv.at[3], to).start()
        gate_buf[:, cols(whole_head(x, y))] = full_low[...]
        took(gate_buf.at[:, 0 : 15 * DH], gate_recv.at[3])
        mine = gate_buf.at[:, 0:split]
        remote(mine, mine, gate_send.at[4], gate_recv.at[4], other_core).start()
        took(gate_buf.at[:, split:], gate_recv.at[4])

    @pl.when(core == 1)
    def _():
        for j in range(1, 16):
            to = place(z, lax.rem(x + j % 4, 4), lax.rem(y + j // 4, 4), core)
            dst = gate_buf.at[at_half, cols(shared_head(x, y))]
            remote(full_low.at[at_half, :], dst, gate_send.at[3], gate_recv.at[3], to).start()
        gate_buf[at_half, cols(shared_head(x, y))] = full_low[at_half, :]
        took(gate_buf.at[0:half, 0 : 15 * DH], gate_recv.at[3])
        mine = gate_buf.at[:, split:]
        remote(mine, mine, gate_send.at[4], gate_recv.at[4], other_core).start()
        took(gate_buf.at[:, 0:split], gate_recv.at[4])

    out_gate[...] = gate_buf[...].astype(F32)

    @pl.when(core == 0)
    def _():
        took(gate_buf.at[:, 0 : 15 * DH], gate_send.at[3])
        took(gate_buf.at[:, 0:split], gate_send.at[4])

    @pl.when(core == 1)
    def _():
        took(gate_buf.at[0:half, 0 : 15 * DH], gate_send.at[3])
        took(gate_buf.at[:, split:], gate_send.at[4])

    took(pieces.at[0 : group - 1], gate_send.at[1])
    took(full.at[0 : (group - 1) * piece, :], gate_send.at[2])
    for s in range(2):
        took(st_kv.at[:, :, 0 : 7 * DH], in_send.at[s])
        took(st_kv.at[:, :, 0 : 7 * DH], out_send.at[s])

    @pl.when(stays)
    def _():
        for s in range(2):
            took(st_kv.at[:, :, 0 : 15 * DH], in_send.at[2 + s])
            took(st_kv.at[:, :, 0 : 15 * DH], out_send.at[2 + s])

    @pl.when(jnp.logical_not(stays))
    def _():
        for s in range(2):
            took(st_kv.at[:, :, 0 : 16 * DH], in_send.at[2 + s])
            took(st_kv.at[:, :, 0 : 16 * DH], out_send.at[2 + s])

    took(out_mq, out_recv.at[0])
    took(out_kv, out_recv.at[1])


def fused(nz, spans_a, spans_b, noise, mask, tab_a, tab_b, q, k, v, c):
    vmem = pl.BlockSpec(memory_space=pltpu.VMEM)
    hbm = pl.BlockSpec(memory_space=pl.ANY)
    block, width = q.shape
    spans = mask.shape[0]
    levels = tab_a.shape[0]
    piece = levels // (2 * nz)

    def low(*shape):
        return pltpu.VMEM(shape, BF16)

    def wide(*shape):
        return pltpu.VMEM(shape, F32)

    def sems(n):
        return pltpu.SemaphoreType.DMA((n,))

    rows_a, rows_b = QA + WINDOW + SPAN, QB + WINDOW + SPAN
    return pl.pallas_call(
        functools.partial(kernel, nz),
        out_shape=[
            jax.ShapeDtypeStruct((2, block, width), BF16),
            jax.ShapeDtypeStruct((2, block, width), BF16),
            jax.ShapeDtypeStruct((levels, width), F32),
        ],
        in_specs=[vmem] * 6 + [hbm] * 4,
        out_specs=[hbm, hbm, vmem],
        scratch_shapes=[
            low(2, block, width), low(2, block, width),
            low(2, rows_a, DH), low(2, rows_b, DH), low(2, QA, DH), low(2, QB, DH),
            low(rows_a, spans),
            wide(QA // TILE, SLAB, TILE), wide(QB // TILE, SLAB, TILE),
            wide(QA, DH), wide(QB, DH), low(levels, QA), low(levels, QB),
            wide(2, rows_a, DH), wide(2, rows_b, DH),
            low(2, QA, DH), low(2, QB, DH), low(2, QA, DH), low(2, QB, DH),
            low(2, WINDOW, DH), low(2, WINDOW, DH), low(2, SPAN, DH), low(2, SPAN, DH),
            low(2, WINDOW, DH), low(2, WINDOW, DH), low(2, SPAN, DH), low(2, SPAN, DH),
            wide(2, levels, DH), wide(levels, DH), wide(2, levels, DH),
            wide(2 * nz, 2, piece, DH), wide(2, piece, DH), wide(levels, DH),
            low(levels, DH), low(levels, width),
            sems(4), sems(4), sems(4), sems(4), sems(4), sems(4), sems(4), sems(4), sems(2),
            sems(5), sems(5),
        ],
        compiler_params=pltpu.CompilerParams(
            collective_id=0, has_side_effects=True, vmem_limit_bytes=60 * 1024 * 1024
        ),
    )(spans_a, spans_b, noise, mask, tab_a, tab_b, q, k, v, c)


def per_device(queries, key_rows, value_rows, out_cotangent, gate_table, span_ids, noise_level, block_mask):
    nz = lax.axis_size("ctx") // 4
    z, x, y, core = where_am_i()
    padded = jnp.pad(span_ids, (WINDOW, SPAN), constant_values=-1)
    start_a = z * PLANE + core * QA
    start_b = z * PLANE + (lax.rem(x, 2) * 2 + core) * QB
    spans_a = lax.dynamic_slice_in_dim(padded, start_a, QA + WINDOW + SPAN, 0)[None, :]
    spans_b = lax.dynamic_slice_in_dim(padded, start_b, QB + WINDOW + SPAN, 0)[None, :]
    tab_a = lax.dynamic_slice_in_dim(gate_table, whole_head(x, y) * DH, DH, 1)
    tab_b = lax.dynamic_slice_in_dim(gate_table, shared_head(x, y) * DH, DH, 1)
    mq, kv, gate_grad = fused(
        nz, spans_a, spans_b, noise_level[None, :], block_mask, tab_a, tab_b,
        queries, key_rows, value_rows, out_cotangent,
    )
    return mq[0], mq[1], kv[0], kv[1], gate_grad


def solution(mesh):
    split = P(("ctx", "head"), None)
    return jax.shard_map(
        per_device,
        mesh=mesh,
        in_specs=(split, split, split, split, P(), P(), P(), P()),
        out_specs=(split, split, split, split, P()),
        check_vma=False,
    )
```

time: 422 us -> 122 us (0.29)
  waiting for transfers between devices: 283 us -> 0 us
  Pallas kernels: 32.5 us -> 112 us
  blocking collectives: 28.6 us -> 0 us
  starting transfers between devices: 22.4 us -> 0 us
  local copies, waits for them, and re-layouts: 31.4 us -> 9.17 us
  between operations: 14.2 us -> 0.7 us
  other arithmetic: 9.12 us -> 0 us
    psum x1 -> x0, waiting for transfers between devices: 209 us -> none  [per_device(): gate_sum = lax.psum(gate_part, 'ctx')]
    pallas_call x1, Pallas kernels: 32.5 us -> 112 us  [fused(): pl.pallas_call(functools.partial(kernel, nz), out_shape=[jax.ShapeDtypeSt...]
    all_gather x1 -> x0, waiting for transfers between devices: 29.2 us -> none  [per_device(): gate_grad = lax.all_gather(gate_sum, 'head', axis=0, tiled=True)]
    all_to_all x1 -> x0, blocking collectives: 28.6 us -> none  [to_heads(): x = lax.all_to_all(x, 'head', 0, 0, tiled=True)]
    all_to_all x3 -> x0, waiting for transfers between devices: 25.5 us -> none  [the longest x1 25.5 us: to_heads(): x = lax.all_to_all(x, 'head', 0, 0, tiled=True)]
    ppermute x4 -> x0, waiting for transfers between devices: 19.3 us -> none  [shifted(): return lax.ppermute(x, 'ctx', [(i, (i + by) % n) for i in range(n)])]
    all_to_all x3 -> x0, starting transfers between devices: 17.3 us -> none  [the longest x2 12.9 us: to_tokens(): x = lax.all_to_all(x, 'head', 0, 0, tiled=True)]
    unnamed x16 -> x3, local copies, waits for them, and re-layouts: 14.1 us -> 1.15 us
  transfers between devices with their start and end apart: 9 -> 0, of which waited for: 4 -> 0; matrix products, arithmetic and copies ran while one was open for 7% -> 0% of each run, Pallas kernels for 0% -> 0%
where the time goes in v2:
time: 122 us
  Pallas kernels  112 us (92%)
  local copies, waits for them, and re-layouts  9.17 us (8%)
    pallas_call x1, Pallas kernels, fused(): pl.pallas_call(functools.partial(kernel, nz), out_shape=[jax.ShapeDtypeSt...  112 us
    squeeze x1, local copies, waits for them, and re-layouts, per_device(): return (mq[0], mq[1], kv[0], kv[1], gate_grad)  3.67 us

profile of v2, /device:TPU:1, one launch (start us, length us, event | category | flops | bytes accessed | tf_op | source)
XLA Modules:
  0.0 121.6 jit_solution(10028948674979056120)
XLA Ops:
  0.7 0.8 pad_dynamic-slice_fusion
  1.5 0.6 broadcast_in_dim.10.span_b
  2.1 0.8 pad_dynamic-slice_fusion.1
  2.9 0.6 broadcast_in_dim.9.span_a
  3.5 1.5 %constant_dynamic-slice_fusion = (f32[128,128]{1,0:T(8,128)}, f32[128,128]{1,0:T(8,128)}) fusion(f32[128,3072]{1,0:T(8,128)} %param.12, s32[]{:T(128)S(6)} %select_n.15, s32[]{:T(128)S(6)} %select_n.14), kind=kLoop, calls=%fused_computation.6 | loop fusion | bytes 262152 | tf_op jit(solution)/shard_map/dynamic_slice | solution.py:534
  5.0 111.7 %shard_map.119 = (bf16[2,128,3072]{2,1,0:T(8,128)(2,1)}, bf16[2,128,3072]{2,1,0:T(8,128)(2,1)}, f32[128,3072]{1,0:T(8,128)}) custom-call(s32[1,3328]{1,0:T(1,128)} %broadcast_in_dim.9.span_a, s32[1,2304]{1,0:T(1,128)} %broadcast_in_dim.10.span_b, s32[1,192]{1,0:T(1,128)} %bitcast.9, s32[192,192]{1,0:T(8,128)} %mask_ref.1, ...), custom_call_target="tpu_custom_call" | custom-call | tf_op jit(solution)/shard_map/pallas_call | solution.py:494
  116.8 0.0 copy-start
  116.8 3.7 %slice_bitcast_fusion = (bf16[128,3072]{1,0:T(8,128)(2,1)}, bf16[128,3072]{1,0:T(8,128)(2,1)}, bf16[128,3072]{1,0:T(8,128)(2,1)}, bf16[128,3072]{1,0:T(8,128)(2,1)}) fusion(bf16[2,128,3072]{2,1,0:T(8,128)(2,1)} %get-tuple-element.9, bf16[2,128,3072]{2,1,0:T(8,128)(2,1)} %get-tuple-element.8), kind=kLoop, calls=%fused_computation | loop fusion | bytes 6291456 | tf_op jit(solution)/shard_map/squeeze | solution.py:539
  120.5 0.0 copy-done
  120.5 1.1 copy.14
Async XLA Ops:
  116.8 3.7 %copy-start = (f32[128,3072]{1,0:T(8,128)S(1)}, f32[128,3072]{1,0:T(8,128)}, u32[]{:S(2)}) copy-start(f32[128,3072]{1,0:T(8,128)} %get-tuple-element.28) | copy-start | bytes 4718596

commit v3 on v2

v3 whole, which is shorter than its diff:
```python
import functools
import math

import jax
import jax.numpy as jnp
from jax import lax
from jax.experimental import pallas as pl
from jax.experimental.pallas import tpu as pltpu
from jax.sharding import PartitionSpec as P

DH = 128
SPAN = 256
WINDOW = 1024
TILE = 256
BLOCK = 128
SLAB = WINDOW + TILE + SPAN
QA = 2 * WINDOW
QB = WINDOW
PLANE = 4 * WINDOW
SCALE = 1.0 / math.sqrt(DH)
LOG2E = 1.0 / math.log(2.0)
HIDDEN = -1e30
F32 = jnp.float32
BF16 = jnp.bfloat16
MESH = pl.DeviceIdType.MESH


def mm(a, b, contract=((1,), (0,))):
    return lax.dot_general(a, b, (contract, ((), ())), preferred_element_type=F32)


def place(z, x, y, core):
    return (z * 4 + lax.rem(x, 2) * 2 + core, lax.div(x, 2) * 4 + y)


def where_am_i():
    ctx = lax.axis_index("ctx")
    head = lax.axis_index("head")
    z = lax.div(ctx, 4)
    x = lax.div(head, 4) * 2 + lax.rem(lax.div(ctx, 2), 2)
    return z, x, lax.rem(head, 4), lax.rem(ctx, 2)


def whole_head(x, y):
    return y * 4 + x


def shared_head(x, y):
    return 16 + y * 2 + lax.div(x, 2)


def prepare(start, span_ref, noise_ref, mask_ref, tab_ref, spans_t, spans_k, bias, gate, level_t):
    spans = mask_ref.shape[0]
    levels = tab_ref.shape[0]
    queries = bias.shape[0] * TILE
    rows = queries + WINDOW + SPAN
    total = span_ref.shape[0]
    first = lax.div(start, BLOCK) - WINDOW // BLOCK
    row = lax.broadcasted_iota(jnp.int32, (spans, BLOCK), 0)

    def encode(i, carry):
        block = first + i
        inside = jnp.logical_and(block >= 0, block < total)
        ids = span_ref[pl.ds(lax.rem(block + total, total), 1), :]
        onehot = (jnp.where(inside, ids, -1) == row).astype(F32)
        at = pl.ds(pl.multiple_of(i * BLOCK, BLOCK), BLOCK)
        spans_t[:, at] = onehot.astype(BF16)
        spans_k[at, :] = onehot.T.astype(BF16)
        return carry

    lax.fori_loop(0, rows // BLOCK, encode, 0)
    own = spans_t[:, WINDOW : WINDOW + queries]
    qs = lax.broadcasted_iota(jnp.int32, (spans, spans), 0)
    ks = lax.broadcasted_iota(jnp.int32, (spans, spans), 1)
    allowed = jnp.where(ks <= qs, mask_ref[...], 0).astype(F32).T.astype(BF16)
    mask_t = mm(allowed, own).astype(BF16)
    k_pos = lax.broadcasted_iota(jnp.int32, (TILE, TILE), 0)
    q_pos = lax.broadcasted_iota(jnp.int32, (TILE, TILE), 1)
    for t in range(bias.shape[0]):
        seen = mm(spans_k[t * TILE : t * TILE + SLAB, :], mask_t[:, t * TILE : (t + 1) * TILE])
        shown = jnp.where(seen > 0.5, 0.0, HIDDEN)
        bias[t, TILE:, :] = shown[TILE:, :]
        bias[t, 0:TILE, :] = jnp.where(k_pos > q_pos, shown[0:TILE, :], HIDDEN)
    lev = lax.broadcasted_iota(jnp.int32, (levels, spans), 0)
    span_level = (noise_ref[...] == lev).astype(BF16)
    level_t[...] = mm(span_level, own).astype(BF16)
    level = mm(spans_k[WINDOW : WINDOW + queries, :], span_level, ((1,), (1,))).astype(BF16)
    table = tab_ref[...]
    high = table.astype(BF16)
    low = (table - high.astype(F32)).astype(BF16)
    gate[...] = mm(level, high) + mm(level, low)


FAR_FIRST = sorted(
    ((jx, jy) for jy in range(4) for jx in range(4)),
    key=lambda j: -(min(j[0], 4 - j[0]) + min(j[1], 4 - j[1])),
)


def attend_tile(t, kv, qg, bias, gate, level_t, acc, res, level_sum):
    q_at = pl.ds(pl.multiple_of(t * TILE, TILE), TILE)
    k_at = pl.ds(pl.multiple_of(t * TILE, TILE), SLAB)
    k = kv[0, k_at, :]
    v = kv[1, k_at, :]
    q = qg[0, q_at, :]
    cot = qg[1, q_at, :].astype(F32)
    gate_rows = gate[q_at, :]
    g_t = (gate_rows * cot).astype(BF16).astype(F32).T
    z = mm(k, q, ((1,), (1,))) * (SCALE * LOG2E) + bias[t]
    top = jnp.max(z, axis=0, keepdims=True)
    e = jnp.exp2(z - top)
    inv = 1.0 / jnp.sum(e, axis=0, keepdims=True)
    e_low = e.astype(BF16)
    att_t = (mm(v, e_low, ((0,), (0,))) * inv).astype(BF16).astype(F32)
    dot = jnp.sum(g_t * att_t, axis=0, keepdims=True) * inv
    gs_t = (g_t * inv).astype(BF16)
    att = att_t.T
    d_prob = mm(v, gs_t)
    ds = (e * (d_prob - dot)).astype(BF16)
    acc[1, k_at, :] += mm(e_low, gs_t, ((1,), (1,)))
    acc[0, k_at, :] += mm(ds, q)
    dq_t = mm(k, ds, ((0,), (0,))) * SCALE
    res[0, q_at, :] = (gate_rows * att).astype(BF16)
    res[1, q_at, :] = dq_t.T.astype(BF16)
    prod = cot * att
    high = prod.astype(BF16)
    low = (prod - high.astype(F32)).astype(BF16)
    lev = level_t[:, q_at]
    level_sum[...] += mm(lev, high) + mm(lev, low)


def kernel(
    nz, span_ref, noise_ref, mask_ref, tab_ref, q_ref, k_ref, v_ref, c_ref,
    out_mq, out_kv, gate_buf,
    st_kv, st_qg, kv_a, kv_b, qg_a, qg_b, tab_a, tab_b, spans_t, spans_k, bias_a, bias_b, gate_a, gate_b, lev_a, lev_b,
    acc_a, acc_b, res_a, res_b, dkv_a, dkv_b, sb_a, sb_b, sa_a, sa_b, rb_a, rb_b, ra_a, ra_b,
    gate_part, gate_pair, gate_core, gate_all, pieces, sums, full, full_low,
    load_sem, in_send, in_recv, halo_send, halo_recv, part_send, part_recv, out_send, out_recv,
    gate_send, gate_recv,
):
    z, x, y, core = where_am_i()
    x_lo = lax.rem(x, 2)
    own_block = lax.div(x, 2) * 4 + y
    stays = core == x_lo
    pair_x = x + 1 - 2 * x_lo
    odd = lax.rem(z, 2)
    half = x_lo + odd - 2 * x_lo * odd
    piece = sums.shape[0]

    def remote(src, dst, send, recv, to):
        return pltpu.make_async_remote_copy(
            src_ref=src, dst_ref=dst, send_sem=send, recv_sem=recv, device_id=to, device_id_type=MESH
        )

    def took(ref, sem):
        pltpu.make_async_copy(ref, ref, sem).wait()

    def cols(head):
        return pl.ds(pl.multiple_of(head * DH, DH), DH)

    def rows(start, size):
        return pl.ds(pl.multiple_of(start, BLOCK), size)

    loads = [
        pltpu.make_async_copy(src, st.at[i], load_sem.at[n])
        for n, (src, st, i) in enumerate(
            ((k_ref, st_kv, 0), (v_ref, st_kv, 1), (q_ref, st_qg, 0), (c_ref, st_qg, 1))
        )
    ]
    loads += [
        pltpu.make_async_copy(tab_ref.at[:, cols(head)], tab, load_sem.at[n])
        for n, head, tab in ((4, whole_head(x, y), tab_a), (5, shared_head(x, y), tab_b))
    ]
    for load in loads:
        load.start()

    barrier = pltpu.get_barrier_semaphore()
    spot = x * 8 + y * 2 + core

    def greet_plane(j, carry):
        other = lax.rem(spot + j, 32)
        to = place(z, lax.div(other, 8), lax.rem(lax.div(other, 2), 4), lax.rem(other, 2))
        pl.semaphore_signal(barrier, inc=1, device_id=to, device_id_type=MESH)
        return carry

    lax.fori_loop(1, 32, greet_plane, 0)

    def greet_column(j, carry):
        to = place(lax.rem(z + j, nz), x, y, core)
        pl.semaphore_signal(barrier, inc=1, device_id=to, device_id_type=MESH)
        return carry

    lax.fori_loop(1, nz, greet_column, 0)
    beyond = lax.rem(z + nz - 1 + 2 * core, nz)
    pl.semaphore_signal(barrier, inc=1, device_id=place(beyond, x, y, 1 - core), device_id_type=MESH)
    pl.semaphore_wait(barrier, 31 + nz)

    def send_shared(st, dst, s):
        start = own_block * BLOCK
        at = dst.at[:, rows(WINDOW + start if dst is kv_b else start, BLOCK), :]
        for jx, jy in ((2, 2), (0, 2), (2, 1), (0, 3), (2, 3), (0, 1), (2, 0), (0, 0)):
            tx = lax.rem(x + jx + odd, 4)
            ty = lax.rem(y + jy, 4)
            src = st.at[:, :, cols(shared_head(tx, ty))]
            go = remote(src, at, in_send.at[s], in_recv.at[s], place(z, tx, ty, core))
            if (jx, jy) == (0, 0):
                @pl.when(odd == 0)
                def _():
                    pltpu.make_async_copy(src, at, in_recv.at[s]).start()

                @pl.when(odd == 1)
                def _():
                    go.start()
            else:
                go.start()

    def send_whole(st, dst, s, order=FAR_FIRST):
        start = core * WINDOW + own_block * BLOCK
        at = dst.at[:, rows(WINDOW + start if dst is kv_a else start, BLOCK), :]
        for jx, jy in order:
            tx = lax.rem(x + jx, 4)
            ty = lax.rem(y + jy, 4)
            src = st.at[:, :, cols(whole_head(tx, ty))]
            go = remote(src, at, in_send.at[s], in_recv.at[s], place(z, tx, ty, x_lo))
            if (jx, jy) == (0, 0):
                @pl.when(stays)
                def _():
                    pltpu.make_async_copy(src, at, in_recv.at[s]).start()

                @pl.when(jnp.logical_not(stays))
                def _():
                    go.start()
            else:
                go.start()

    loads[0].wait()
    loads[1].wait()
    send_shared(st_kv, kv_b, 0)
    loads[2].wait()
    loads[3].wait()
    send_shared(st_qg, qg_b, 1)

    loads[4].wait()
    loads[5].wait()
    start_a = z * PLANE + core * QA
    start_b = z * PLANE + (half * 2 + core) * QB
    prepare(start_b, span_ref, noise_ref, mask_ref, tab_b, spans_t, spans_k, bias_b, gate_b, lev_b)
    acc_b[...] = jnp.zeros_like(acc_b)
    gate_part[...] = jnp.zeros_like(gate_part)

    next_a = place(lax.rem(z + core, nz), x, y, 1 - core)
    prev_a = place(lax.rem(z + nz - 1 + core, nz), x, y, 1 - core)
    next_b = place(
        lax.rem(z + core * half, nz), jnp.where(core * (1 - half) == 1, pair_x, x), y, 1 - core
    )
    prev_b = place(
        lax.rem(z + nz - (1 - core) * (1 - half), nz),
        jnp.where((1 - core) * half == 1, pair_x, x),
        y,
        1 - core,
    )

    def halo(kv, queries, n, after, before):
        last = WINDOW + queries
        return (
            remote(
                kv.at[:, queries:last, :], kv.at[:, 0:WINDOW, :], halo_send.at[n], halo_recv.at[n], after
            ),
            remote(
                kv.at[:, WINDOW : WINDOW + SPAN, :],
                kv.at[:, last : last + SPAN, :],
                halo_send.at[n + 1],
                halo_recv.at[n + 1],
                before,
            ),
        )

    halo_b = halo(kv_b, QB, 0, next_b, prev_b)
    halo_a = halo(kv_a, QA, 2, next_a, prev_a)

    took(kv_b.at[:, WINDOW : WINDOW + QB, :], in_recv.at[0])
    for c in halo_b:
        c.start()
    send_whole(st_kv, kv_a, 2)
    prepare(start_a, span_ref, noise_ref, mask_ref, tab_a, spans_t, spans_k, bias_a, gate_a, lev_a)
    acc_a[...] = jnp.zeros_like(acc_a)
    took(qg_b, in_recv.at[1])
    send_whole(st_qg, qg_a, 3, FAR_FIRST[:8])
    for c in halo_b:
        c.wait()

    def give_shared(buf, out, i, s):
        src = buf.at[:, rows(i * BLOCK, BLOCK), :]
        dst = out.at[:, :, cols(shared_head(x, y))]
        mine = jnp.logical_and(odd == 0, i == own_block)

        @pl.when(mine)
        def _():
            pltpu.make_async_copy(src, dst, out_recv.at[s]).start()

        @pl.when(jnp.logical_not(mine))
        def _():
            to = place(z, lax.div(i, 4) * 2 + half, lax.rem(i, 4), core)
            remote(src, dst, out_send.at[s], out_recv.at[s], to).start()

    def give_whole(buf, out, i, s):
        src = buf.at[:, rows(i * BLOCK, BLOCK), :]
        dst = out.at[:, :, cols(whole_head(x, y))]
        mine = jnp.logical_and(stays, i == core * 8 + own_block)

        @pl.when(mine)
        def _():
            pltpu.make_async_copy(src, dst, out_recv.at[s]).start()

        @pl.when(jnp.logical_not(mine))
        def _():
            b = lax.rem(i, 8)
            to = place(z, lax.div(b, 4) * 2 + core, lax.rem(b, 4), lax.div(i, 8))
            remote(src, dst, out_send.at[2 + s], out_recv.at[s], to).start()

    turn = lax.div(own_block, 2) + 1

    def tile_b(step, carry):
        t = lax.rem(turn + step, QB // TILE)
        attend_tile(t, kv_b, qg_b, bias_b, gate_b, lev_b, acc_b, res_b, gate_part.at[1])
        return carry

    lax.fori_loop(0, QB // TILE, tile_b, 0)

    def part(buf, recv, n, to):
        return remote(buf, recv, part_send.at[n], part_recv.at[n], to)

    behind_b = part(sb_b, rb_b, 0, prev_b)
    ahead_b = part(sa_b, ra_b, 1, next_b)
    behind_a = part(sb_a, rb_a, 2, prev_a)
    ahead_a = part(sa_a, ra_a, 3, next_a)
    pair_gate = remote(
        gate_part.at[1], gate_pair, gate_send.at[0], gate_recv.at[0], place(z, pair_x, y, core)
    )

    for i, s in ((0, SCALE), (1, 1.0)):
        sb_b[i] = (acc_b[i, 0:WINDOW, :] * s).astype(BF16)
        sa_b[i] = (acc_b[i, WINDOW + QB :, :] * s).astype(BF16)
    took(kv_a.at[:, WINDOW : WINDOW + QA, :], in_recv.at[2])
    for c in halo_a:
        c.start()
    send_whole(st_qg, qg_a, 3, FAR_FIRST[8:])
    behind_b.start()
    ahead_b.start()
    pair_gate.start()

    def give_mixed(j, carry):
        give_shared(res_b, out_mq, lax.rem(own_block + 1 + j, QB // BLOCK), 0)
        return carry

    lax.fori_loop(0, QB // BLOCK, give_mixed, 0)
    took(qg_a, in_recv.at[3])
    for c in halo_a:
        c.wait()

    def finish_b():
        behind_b.wait()
        ahead_b.wait()
        for i, s in ((0, SCALE), (1, 1.0)):
            total = acc_b[i, WINDOW : WINDOW + QB, :] * s + rb_b[i].astype(F32)
            dkv_b[i] = total.astype(BF16)
            first = total[0:SPAN, :] + ra_b[i].astype(F32)
            dkv_b[i, 0:SPAN, :] = first.astype(BF16)

        def give(j, carry):
            give_shared(dkv_b, out_kv, lax.rem(own_block + 1 + j, QB // BLOCK), 1)
            return carry

        lax.fori_loop(0, QB // BLOCK, give, 0)

    def tile_a(step, carry):
        t = lax.div(step, 4) * 4 + lax.rem(turn + step, 4)
        attend_tile(t, kv_a, qg_a, bias_a, gate_a, lev_a, acc_a, res_a, gate_part.at[0])
        for j in range(TILE // BLOCK):
            give_whole(res_a, out_mq, t * (TILE // BLOCK) + j, 0)

        @pl.when(step == 1)
        def _():
            finish_b()

        @pl.when(step == 3)
        def _():
            for i, s in ((0, SCALE), (1, 1.0)):
                sb_a[i] = (acc_a[i, 0:WINDOW, :] * s).astype(BF16)
            behind_a.start()

        return carry

    lax.fori_loop(0, QA // TILE, tile_a, 0)

    for i, s in ((0, SCALE), (1, 1.0)):
        sa_a[i] = (acc_a[i, WINDOW + QA :, :] * s).astype(BF16)
    ahead_a.start()

    pair_gate.wait()
    gate_part[1] = gate_part[1] + gate_pair[...]
    other_core = place(z, x, y, 1 - core)
    core_gate = remote(
        gate_part.at[1 - core], gate_core, gate_send.at[1], gate_recv.at[1], other_core
    )
    core_gate.start()

    behind_a.wait()
    for i, s in ((0, SCALE), (1, 1.0)):
        own = acc_a[i, WINDOW + SPAN : 2 * WINDOW, :] * s
        dkv_a[i, SPAN:WINDOW, :] = own.astype(BF16)
        total = acc_a[i, 2 * WINDOW : 2 * WINDOW + WINDOW, :] * s + rb_a[i].astype(F32)
        dkv_a[i, WINDOW:, :] = total.astype(BF16)

    def give_rest(j, carry):
        i = lax.rem(core * 8 + own_block + 1 + j, QA // BLOCK)

        @pl.when(i >= SPAN // BLOCK)
        def _():
            give_whole(dkv_a, out_kv, i, 1)

        return carry

    core_gate.wait()
    gate_all[...] = gate_part[core] + gate_core[...]
    at_mine = pl.ds(pl.multiple_of(z * piece, piece), piece)

    def to_column(j, carry):
        other = lax.rem(z + j, nz)
        src = gate_all.at[pl.ds(pl.multiple_of(other * piece, piece), piece), :]
        to = place(other, x, y, core)
        remote(src, pieces.at[z], gate_send.at[2], gate_recv.at[2], to).start()
        return carry

    lax.fori_loop(1, nz, to_column, 0)
    lax.fori_loop(0, QA // BLOCK, give_rest, 0)

    took(pieces.at[0 : nz - 1], gate_recv.at[2])
    total = gate_all[at_mine, :]
    for j in range(1, nz):
        total = total + pieces[lax.rem(z + j, nz)]
    sums[...] = total
    full[at_mine, :] = total

    def back_to_column(j, carry):
        to = place(lax.rem(z + j, nz), x, y, core)
        remote(sums, full.at[at_mine, :], gate_send.at[3], gate_recv.at[3], to).start()
        return carry

    lax.fori_loop(1, nz, back_to_column, 0)

    ahead_a.wait()
    for i, s in ((0, SCALE), (1, 1.0)):
        first = acc_a[i, WINDOW : WINDOW + SPAN, :] * s + ra_a[i].astype(F32)
        dkv_a[i, 0:SPAN, :] = first.astype(BF16)
    def give_first(i, carry):
        give_whole(dkv_a, out_kv, i, 1)
        return carry

    lax.fori_loop(0, SPAN // BLOCK, give_first, 0)

    took(full.at[0 : (nz - 1) * piece, :], gate_recv.at[3])
    split = whole_head(0, 4) * DH
    half_rows = DH // 2
    low_rows = pl.ds(pl.multiple_of(x_lo * half_rows, half_rows), half_rows)
    row_a = pl.ds(pl.multiple_of(y * 4 * DH, DH), 4 * DH)
    row_b = pl.ds(pl.multiple_of(split + y * 2 * DH, DH), 2 * DH)
    full_low[...] = full[...].astype(BF16)

    def spread_gate(mine, row, one, three, all_rows, theirs):
        for jx in range(1, 4):
            to = place(z, lax.rem(x + jx, 4), y, core)
            remote(mine[0], mine[1], gate_send.at[4], gate_recv.at[4], to).start()
        took(one, gate_recv.at[4])
        for jy in range(1, 4):
            to = place(z, x, lax.rem(y + jy, 4), core)
            remote(row, row, gate_send.at[5], gate_recv.at[5], to).start()
        took(three, gate_recv.at[5])
        remote(all_rows, all_rows, gate_send.at[6], gate_recv.at[6], other_core).start()
        took(theirs, gate_recv.at[6])
        took(one, gate_send.at[4])
        took(three, gate_send.at[5])
        took(all_rows, gate_send.at[6])

    whole = gate_buf.at[:, 0:split]
    shared = gate_buf.at[:, split:]

    @pl.when(core == 0)
    def _():
        at = cols(whole_head(x, y))
        gate_buf[:, at] = full_low[...]
        spread_gate(
            (full_low, gate_buf.at[:, at]), gate_buf.at[:, row_a],
            gate_buf.at[:, 0 : 3 * DH], gate_buf.at[:, 0 : 12 * DH], whole, shared,
        )

    @pl.when(core == 1)
    def _():
        at = cols(shared_head(x, y))
        gate_buf[low_rows, at] = full_low[low_rows, :]
        spread_gate(
            (full_low.at[low_rows, :], gate_buf.at[low_rows, at]), gate_buf.at[:, row_b],
            gate_buf.at[0:half_rows, 0 : 3 * DH], gate_buf.at[:, 0 : 6 * DH], shared, whole,
        )

    took(pieces.at[0 : nz - 1], gate_send.at[2])
    took(full.at[0 : (nz - 1) * piece, :], gate_send.at[3])

    @pl.when(odd == 0)
    def _():
        for s in range(2):
            took(st_kv.at[:, :, 0 : 7 * DH], in_send.at[s])
            took(st_kv.at[:, :, 0 : 7 * DH], out_send.at[s])

    @pl.when(odd == 1)
    def _():
        for s in range(2):
            took(st_kv.at[:, :, 0 : 8 * DH], in_send.at[s])
            took(st_kv.at[:, :, 0 : 8 * DH], out_send.at[s])

    @pl.when(stays)
    def _():
        for s in range(2):
            took(st_kv.at[:, :, 0 : 15 * DH], in_send.at[2 + s])
            took(st_kv.at[:, :, 0 : 15 * DH], out_send.at[2 + s])

    @pl.when(jnp.logical_not(stays))
    def _():
        for s in range(2):
            took(st_kv.at[:, :, 0 : 16 * DH], in_send.at[2 + s])
            took(st_kv.at[:, :, 0 : 16 * DH], out_send.at[2 + s])

    took(out_mq, out_recv.at[0])
    took(out_kv, out_recv.at[1])


def fused(nz, span_rows, noise, mask, table, q, k, v, c):
    vmem = pl.BlockSpec(memory_space=pltpu.VMEM)
    hbm = pl.BlockSpec(memory_space=pl.ANY)
    block, width = q.shape
    spans = mask.shape[0]
    levels = table.shape[0]
    piece = levels // nz

    def low(*shape):
        return pltpu.VMEM(shape, BF16)

    def wide(*shape):
        return pltpu.VMEM(shape, F32)

    def sems(n):
        return pltpu.SemaphoreType.DMA((n,))

    rows_a, rows_b = QA + WINDOW + SPAN, QB + WINDOW + SPAN
    return pl.pallas_call(
        functools.partial(kernel, nz),
        out_shape=[
            jax.ShapeDtypeStruct((2, block, width), BF16),
            jax.ShapeDtypeStruct((2, block, width), BF16),
            jax.ShapeDtypeStruct((levels, width), BF16),
        ],
        in_specs=[vmem] * 3 + [hbm] * 5,
        out_specs=[hbm, hbm, vmem],
        scratch_shapes=[
            low(2, block, width), low(2, block, width),
            low(2, rows_a, DH), low(2, rows_b, DH), low(2, QA, DH), low(2, QB, DH),
            wide(levels, DH), wide(levels, DH),
            low(spans, rows_a), low(rows_a, spans),
            wide(QA // TILE, SLAB, TILE), wide(QB // TILE, SLAB, TILE),
            wide(QA, DH), wide(QB, DH), low(levels, QA), low(levels, QB),
            wide(2, rows_a, DH), wide(2, rows_b, DH),
            low(2, QA, DH), low(2, QB, DH), low(2, QA, DH), low(2, QB, DH),
            low(2, WINDOW, DH), low(2, WINDOW, DH), low(2, SPAN, DH), low(2, SPAN, DH),
            low(2, WINDOW, DH), low(2, WINDOW, DH), low(2, SPAN, DH), low(2, SPAN, DH),
            wide(2, levels, DH), wide(levels, DH), wide(levels, DH), wide(levels, DH),
            wide(nz, piece, DH), wide(piece, DH), wide(levels, DH), low(levels, DH),
            sems(6), sems(4), sems(4), sems(4), sems(4), sems(4), sems(4), sems(4), sems(2),
            sems(7), sems(7),
        ],
        compiler_params=pltpu.CompilerParams(
            collective_id=0, has_side_effects=True, vmem_limit_bytes=60 * 1024 * 1024
        ),
    )(span_rows, noise, mask, table, q, k, v, c)


def per_device(queries, key_rows, value_rows, out_cotangent, gate_table, span_ids, noise_level, block_mask):
    nz = lax.axis_size("ctx") // 4
    mq, kv, gate_low = fused(
        nz, span_ids.reshape(-1, BLOCK), noise_level[None, :], block_mask, gate_table,
        queries, key_rows, value_rows, out_cotangent,
    )
    return mq[0], mq[1], kv[0], kv[1], gate_low.astype(F32)


def solution(mesh):
    split = P(("ctx", "head"), None)
    return jax.shard_map(
        per_device,
        mesh=mesh,
        in_specs=(split, split, split, split, P(), P(), P(), P()),
        out_specs=(split, split, split, split, P()),
        check_vma=False,
    )
```

time: 122 us -> 108 us (0.89)
  Pallas kernels: 112 us -> 102 us
  local copies, waits for them, and re-layouts: 9.17 us -> 3.63 us
  other arithmetic: 0 us -> 1.3 us
    pallas_call x1, Pallas kernels: 112 us -> 102 us  [fused(): pl.pallas_call(functools.partial(kernel, nz), out_shape=[jax.ShapeDtypeSt...]
    dynamic_slice x3 -> x0, local copies, waits for them, and re-layouts: 3.13 us -> none  [the longest x1 1.53 us: per_device(): tab_b = lax.dynamic_slice_in_dim(gate_table, shared_head(x, y) * DH, DH, 1)]
    convert_element_type x0 -> x1, other arithmetic: none -> 1.3 us  [per_device(): return (mq[0], mq[1], kv[0], kv[1], gate_low.astype(F32))]
where the time goes in v3:
time: 108 us
  Pallas kernels  102 us (94%)
  local copies, waits for them, and re-layouts  3.63 us (3%)
  other arithmetic  1.3 us (1%)
    pallas_call x1, Pallas kernels, fused(): pl.pallas_call(functools.partial(kernel, nz), out_shape=[jax.ShapeDtypeSt...  102 us
    squeeze x1, local copies, waits for them, and re-layouts, per_device(): return (mq[0], mq[1], kv[0], kv[1], gate_low.astype(F32))  3.63 us

profile of v3, /device:TPU:1, one launch (start us, length us, event | category | flops | bytes accessed | tf_op | source)
XLA Modules:
  0.0 107.7 jit_solution(2708411743343104265)
XLA Ops:
  0.6 102.1 %shard_map.119 = (bf16[2,128,3072]{2,1,0:T(8,128)(2,1)}, bf16[2,128,3072]{2,1,0:T(8,128)(2,1)}, bf16[128,3072]{1,0:T(8,128)(2,1)}) custom-call(s32[256,128]{1,0:T(8,128)} %bitcast.10, s32[1,192]{1,0:T(1,128)} %bitcast.11, s32[192,192]{1,0:T(8,128)} %mask_ref.1, f32[128,3072]{1,0:T(8,128)} %tab_ref.1, bf16[128,3072]{1,0:T(8,128)(2,1)} %q_ref.1, ...), custom_call_target="tpu_custom_call" | custom-call | tf_op jit(solution)/shard_map/pallas_call | solution.py:555
  102.7 0.0 copy-start
  102.7 3.6 %slice_bitcast_fusion = (bf16[128,3072]{1,0:T(8,128)(2,1)}, bf16[128,3072]{1,0:T(8,128)(2,1)}, bf16[128,3072]{1,0:T(8,128)(2,1)}, bf16[128,3072]{1,0:T(8,128)(2,1)}) fusion(bf16[2,128,3072]{2,1,0:T(8,128)(2,1)} %get-tuple-element.9, bf16[2,128,3072]{2,1,0:T(8,128)(2,1)} %get-tuple-element.8), kind=kLoop, calls=%fused_computation | loop fusion | bytes 6291456 | tf_op jit(solution)/shard_map/squeeze | solution.py:592
  106.4 0.0 copy-done
  106.4 1.3 %convert_element_type.3 = f32[128,3072]{1,0:T(8,128)} convert(bf16[128,3072]{1,0:T(8,128)(2,1)S(1)} %copy-done) | non-fusion elementwise | flops 393216 | bytes 2359296 | tf_op jit(solution)/shard_map/convert_element_type | solution.py:592
Async XLA Ops:
  102.7 3.6 %copy-start = (bf16[128,3072]{1,0:T(8,128)(2,1)S(1)}, bf16[128,3072]{1,0:T(8,128)(2,1)}, u32[]{:S(2)}) copy-start(bf16[128,3072]{1,0:T(8,128)(2,1)} %get-tuple-element.10) | copy-start | bytes 2359300

commit v4 on v3

--- a/solution.py
+++ b/solution.py
@@ -95,6 +95,9 @@
     ((jx, jy) for jy in range(4) for jx in range(4)),
     key=lambda j: -(min(j[0], 4 - j[0]) + min(j[1], 4 - j[1])),
 )
+
+
+HALO_STEP = 1
 
 
 def attend_tile(t, kv, qg, bias, gate, level_t, acc, res, level_sum):
@@ -129,12 +132,49 @@
     level_sum[...] += mm(lev, high) + mm(lev, low)
 
 
+def forward_tile(t, kv, qg, bias, gate, level_t, res, level_sum, exps, scaled, dots):
+    q_at = pl.ds(pl.multiple_of(t * TILE, TILE), TILE)
+    k_at = pl.ds(pl.multiple_of(t * TILE, TILE), SLAB)
+    cot = qg[1, q_at, :].astype(F32)
+    gate_rows = gate[q_at, :]
+    g_t = (gate_rows * cot).astype(BF16).astype(F32).T
+    z = mm(kv[0, k_at, :], qg[0, q_at, :], ((1,), (1,))) * (SCALE * LOG2E) + bias[t]
+    top = jnp.max(z, axis=0, keepdims=True)
+    e = jnp.exp2(z - top)
+    inv = 1.0 / jnp.sum(e, axis=0, keepdims=True)
+    e_low = e.astype(BF16)
+    exps[t] = e_low
+    att_t = (mm(kv[1, k_at, :], e_low, ((0,), (0,))) * inv).astype(BF16).astype(F32)
+    dots[t] = jnp.sum(g_t * att_t, axis=0, keepdims=True) * inv
+    scaled[t] = (g_t * inv).astype(BF16)
+    att = att_t.T
+    res[0, q_at, :] = (gate_rows * att).astype(BF16)
+    prod = cot * att
+    high = prod.astype(BF16)
+    low = (prod - high.astype(F32)).astype(BF16)
+    lev = level_t[:, q_at]
+    level_sum[...] += mm(lev, high) + mm(lev, low)
+
+
+def backward_tile(t, kv, qg, acc, res, exps, scaled, dots):
+    q_at = pl.ds(pl.multiple_of(t * TILE, TILE), TILE)
+    k_at = pl.ds(pl.multiple_of(t * TILE, TILE), SLAB)
+    e_low = exps[t]
+    gs_t = scaled[t]
+    d_prob = mm(kv[1, k_at, :], gs_t)
+    ds = (e_low.astype(F32) * (d_prob - dots[t])).astype(BF16)
+    acc[1, k_at, :] += mm(e_low, gs_t, ((1,), (1,)))
+    acc[0, k_at, :] += mm(ds, qg[0, q_at, :])
+    dq_t = mm(kv[0, k_at, :], ds, ((0,), (0,))) * SCALE
+    res[1, q_at, :] = dq_t.T.astype(BF16)
+
+
 def kernel(
     nz, span_ref, noise_ref, mask_ref, tab_ref, q_ref, k_ref, v_ref, c_ref,
     out_mq, out_kv, gate_buf,
     st_kv, st_qg, kv_a, kv_b, qg_a, qg_b, tab_a, tab_b, spans_t, spans_k, bias_a, bias_b, gate_a, gate_b, lev_a, lev_b,
-    acc_a, acc_b, res_a, res_b, dkv_a, dkv_b, sb_a, sb_b, sa_a, sa_b, rb_a, rb_b, ra_a, ra_b,
-    gate_part, gate_pair, gate_core, gate_all, pieces, sums, full, full_low,
+    acc_a, acc_b, exps, scaled, dots, res_a, res_b, dkv_a, dkv_b, sb_a, sb_b, sa_a, sa_b, rb_a, rb_b, ra_a, ra_b,
+    gate_part, gate_three, gate_core, gate_all, pieces, sums, full, full_low,
     load_sem, in_send, in_recv, halo_send, halo_recv, part_send, part_recv, out_send, out_recv,
     gate_send, gate_recv,
 ):
@@ -233,21 +273,8 @@
             else:
                 go.start()
 
-    loads[0].wait()
-    loads[1].wait()
-    send_shared(st_kv, kv_b, 0)
-    loads[2].wait()
-    loads[3].wait()
-    send_shared(st_qg, qg_b, 1)
-
-    loads[4].wait()
-    loads[5].wait()
     start_a = z * PLANE + core * QA
     start_b = z * PLANE + (half * 2 + core) * QB
-    prepare(start_b, span_ref, noise_ref, mask_ref, tab_b, spans_t, spans_k, bias_b, gate_b, lev_b)
-    acc_b[...] = jnp.zeros_like(acc_b)
-    gate_part[...] = jnp.zeros_like(gate_part)
-
     next_a = place(lax.rem(z + core, nz), x, y, 1 - core)
     prev_a = place(lax.rem(z + nz - 1 + core, nz), x, y, 1 - core)
     next_b = place(
@@ -278,17 +305,6 @@
     halo_b = halo(kv_b, QB, 0, next_b, prev_b)
     halo_a = halo(kv_a, QA, 2, next_a, prev_a)
 
-    took(kv_b.at[:, WINDOW : WINDOW + QB, :], in_recv.at[0])
-    for c in halo_b:
-        c.start()
-    send_whole(st_kv, kv_a, 2)
-    prepare(start_a, span_ref, noise_ref, mask_ref, tab_a, spans_t, spans_k, bias_a, gate_a, lev_a)
-    acc_a[...] = jnp.zeros_like(acc_a)
-    took(qg_b, in_recv.at[1])
-    send_whole(st_qg, qg_a, 3, FAR_FIRST[:8])
-    for c in halo_b:
-        c.wait()
-
     def give_shared(buf, out, i, s):
         src = buf.at[:, rows(i * BLOCK, BLOCK), :]
         dst = out.at[:, :, cols(shared_head(x, y))]
@@ -318,15 +334,6 @@
             to = place(z, lax.div(b, 4) * 2 + core, lax.rem(b, 4), lax.div(i, 8))
             remote(src, dst, out_send.at[2 + s], out_recv.at[s], to).start()
 
-    turn = lax.div(own_block, 2) + 1
-
-    def tile_b(step, carry):
-        t = lax.rem(turn + step, QB // TILE)
-        attend_tile(t, kv_b, qg_b, bias_b, gate_b, lev_b, acc_b, res_b, gate_part.at[1])
-        return carry
-
-    lax.fori_loop(0, QB // TILE, tile_b, 0)
-
     def part(buf, recv, n, to):
         return remote(buf, recv, part_send.at[n], part_recv.at[n], to)
 
@@ -334,29 +341,21 @@
     ahead_b = part(sa_b, ra_b, 1, next_b)
     behind_a = part(sb_a, rb_a, 2, prev_a)
     ahead_a = part(sa_a, ra_a, 3, next_a)
-    pair_gate = remote(
-        gate_part.at[1], gate_pair, gate_send.at[0], gate_recv.at[0], place(z, pair_x, y, core)
-    )
-
-    for i, s in ((0, SCALE), (1, 1.0)):
-        sb_b[i] = (acc_b[i, 0:WINDOW, :] * s).astype(BF16)
-        sa_b[i] = (acc_b[i, WINDOW + QB :, :] * s).astype(BF16)
-    took(kv_a.at[:, WINDOW : WINDOW + QA, :], in_recv.at[2])
-    for c in halo_a:
-        c.start()
-    send_whole(st_qg, qg_a, 3, FAR_FIRST[8:])
-    behind_b.start()
-    ahead_b.start()
-    pair_gate.start()
-
-    def give_mixed(j, carry):
-        give_shared(res_b, out_mq, lax.rem(own_block + 1 + j, QB // BLOCK), 0)
-        return carry
-
-    lax.fori_loop(0, QB // BLOCK, give_mixed, 0)
-    took(qg_a, in_recv.at[3])
-    for c in halo_a:
-        c.wait()
+    def share_gate():
+        def send(x_to, slot):
+            to = place(z, x_to, y, 1)
+            remote(
+                gate_part.at[1], gate_three.at[slot], gate_send.at[0], gate_recv.at[0], to
+            ).start()
+
+        @pl.when(core == 0)
+        def _():
+            send(x, 0)
+            send(pair_x, 1)
+
+        @pl.when(core == 1)
+        def _():
+            send(pair_x, 2)
 
     def finish_b():
         behind_b.wait()
@@ -373,15 +372,138 @@
 
         lax.fori_loop(0, QB // BLOCK, give, 0)
 
+    other_core = place(z, x, y, 1 - core)
+    core_gate = remote(
+        gate_part.at[0], gate_core, gate_send.at[1], gate_recv.at[1], other_core
+    )
+    at_mine = pl.ds(pl.multiple_of(z * piece, piece), piece)
+    split = whole_head(0, 4) * DH
+    half_rows = DH // 2
+    low_rows = pl.ds(pl.multiple_of(x_lo * half_rows, half_rows), half_rows)
+    at_a = cols(whole_head(x, y))
+    at_b = cols(shared_head(x, y))
+    whole = gate_buf.at[:, 0:split]
+    shared = gate_buf.at[:, split:]
+    along_x = (
+        (full_low, gate_buf.at[:, at_a], gate_buf.at[:, 0 : 3 * DH]),
+        (
+            full_low.at[low_rows, :],
+            gate_buf.at[low_rows, at_b],
+            gate_buf.at[0:half_rows, 0 : 3 * DH],
+        ),
+    )
+    along_y = (
+        (gate_buf.at[:, pl.ds(pl.multiple_of(y * 4 * DH, DH), 4 * DH)], gate_buf.at[:, 0 : 12 * DH]),
+        (
+            gate_buf.at[:, pl.ds(pl.multiple_of(split + y * 2 * DH, DH), 2 * DH)],
+            gate_buf.at[:, 0 : 6 * DH],
+        ),
+    )
+    across = ((whole, shared), (shared, whole))
+
+
+    def to_column(c):
+        if c == 0:
+            core_gate.wait_recv()
+            gate_all[...] = gate_part[0] + gate_core[...]
+        else:
+            took(gate_three, gate_recv.at[0])
+            gate_all[...] = gate_part[1] + gate_three[0] + gate_three[1] + gate_three[2]
+
+        def send(j, carry):
+            other = lax.rem(z + j, nz)
+            src = gate_all.at[pl.ds(pl.multiple_of(other * piece, piece), piece), :]
+            to = place(other, x, y, core)
+            remote(src, pieces.at[z], gate_send.at[2], gate_recv.at[2], to).start()
+            return carry
+
+        lax.fori_loop(1, nz, send, 0)
+
+    def back_to_column():
+        took(pieces.at[0 : nz - 1], gate_recv.at[2])
+        total = gate_all[at_mine, :]
+        for j in range(1, nz):
+            total = total + pieces[lax.rem(z + j, nz)]
+        sums[...] = total
+        full[at_mine, :] = total
+
+        def send(j, carry):
+            to = place(lax.rem(z + j, nz), x, y, core)
+            remote(sums, full.at[at_mine, :], gate_send.at[3], gate_recv.at[3], to).start()
+            return carry
+
+        lax.fori_loop(1, nz, send, 0)
+
+    def go_along_x(c):
+        took(full.at[0 : (nz - 1) * piece, :], gate_recv.at[3])
+        full_low[...] = full[...].astype(BF16)
+        if c == 0:
+            gate_buf[:, at_a] = full_low[...]
+        else:
+            gate_buf[low_rows, at_b] = full_low[low_rows, :]
+        src, dst, _ = along_x[c]
+        for jx in range(1, 4):
+            to = place(z, lax.rem(x + jx, 4), y, core)
+            remote(src, dst, gate_send.at[4], gate_recv.at[4], to).start()
+
+    def go_along_y(c):
+        took(along_x[c][2], gate_recv.at[4])
+        mine = along_y[c][0]
+        for jy in range(1, 4):
+            to = place(z, x, lax.rem(y + jy, 4), core)
+            remote(mine, mine, gate_send.at[5], gate_recv.at[5], to).start()
+
+    def go_across(c):
+        took(along_y[c][1], gate_recv.at[5])
+        mine = across[c][0]
+        remote(mine, mine, gate_send.at[6], gate_recv.at[6], other_core).start()
+
+    def last(c):
+        took(across[c][1], gate_recv.at[6])
+        took(along_x[c][2], gate_send.at[4])
+        took(along_y[c][1], gate_send.at[5])
+        took(across[c][0], gate_send.at[6])
+        took(gate_three.at[0 : 2 - c], gate_send.at[0])
+        if c == 1:
+            core_gate.wait_send()
+
+    loads[0].wait()
+    loads[1].wait()
+    send_whole(st_kv, kv_a, 2)
+    loads[2].wait()
+    loads[3].wait()
+    send_whole(st_qg, qg_a, 3, FAR_FIRST[:8])
+    loads[4].wait()
+    loads[5].wait()
+    prepare(start_a, span_ref, noise_ref, mask_ref, tab_a, spans_t, spans_k, bias_a, gate_a, lev_a)
+    acc_a[...] = jnp.zeros_like(acc_a)
+    gate_part[...] = jnp.zeros_like(gate_part)
+    took(kv_a.at[:, WINDOW : WINDOW + QA, :], in_recv.at[2])
+    for c in halo_a:
+        c.start()
+    send_shared(st_kv, kv_b, 0)
+    send_whole(st_qg, qg_a, 3, FAR_FIRST[8:])
+    prepare(start_b, span_ref, noise_ref, mask_ref, tab_b, spans_t, spans_k, bias_b, gate_b, lev_b)
+    acc_b[...] = jnp.zeros_like(acc_b)
+    took(qg_a, in_recv.at[3])
+    for c in halo_a:
+        c.wait()
+    send_shared(st_qg, qg_b, 1)
+
+    turn = lax.div(own_block, 2) + 1
+
     def tile_a(step, carry):
         t = lax.div(step, 4) * 4 + lax.rem(turn + step, 4)
         attend_tile(t, kv_a, qg_a, bias_a, gate_a, lev_a, acc_a, res_a, gate_part.at[0])
+
+        @pl.when(step == HALO_STEP)
+        def _():
+            took(kv_b.at[:, WINDOW : WINDOW + QB, :], in_recv.at[0])
+            for c in halo_b:
+                c.start()
+
         for j in range(TILE // BLOCK):
             give_whole(res_a, out_mq, t * (TILE // BLOCK) + j, 0)
-
-        @pl.when(step == 1)
-        def _():
-            finish_b()
 
         @pl.when(step == 3)
         def _():
@@ -397,13 +519,9 @@
         sa_a[i] = (acc_a[i, WINDOW + QA :, :] * s).astype(BF16)
     ahead_a.start()
 
-    pair_gate.wait()
-    gate_part[1] = gate_part[1] + gate_pair[...]
-    other_core = place(z, x, y, 1 - core)
-    core_gate = remote(
-        gate_part.at[1 - core], gate_core, gate_send.at[1], gate_recv.at[1], other_core
-    )
-    core_gate.start()
+    @pl.when(core == 1)
+    def _():
+        core_gate.start()
 
     behind_a.wait()
     for i, s in ((0, SCALE), (1, 1.0)):
@@ -421,87 +539,98 @@
 
         return carry
 
-    core_gate.wait()
-    gate_all[...] = gate_part[core] + gate_core[...]
-    at_mine = pl.ds(pl.multiple_of(z * piece, piece), piece)
-
-    def to_column(j, carry):
-        other = lax.rem(z + j, nz)
-        src = gate_all.at[pl.ds(pl.multiple_of(other * piece, piece), piece), :]
-        to = place(other, x, y, core)
-        remote(src, pieces.at[z], gate_send.at[2], gate_recv.at[2], to).start()
+    lax.fori_loop(0, QA // BLOCK, give_rest, 0)
+    took(qg_b, in_recv.at[1])
+    for c in halo_b:
+        c.wait()
+
+    def forward_b(step, carry):
+        t = lax.rem(turn + step, QB // TILE)
+        forward_tile(
+            t, kv_b, qg_b, bias_b, gate_b, lev_b, res_b, gate_part.at[1], exps, scaled, dots
+        )
+
+        @pl.when(jnp.logical_and(step == 0, core == 0))
+        def _():
+            to_column(0)
+
+        @pl.when(jnp.logical_and(step == 3, core == 0))
+        def _():
+            back_to_column()
+
         return carry
 
-    lax.fori_loop(1, nz, to_column, 0)
-    lax.fori_loop(0, QA // BLOCK, give_rest, 0)
-
-    took(pieces.at[0 : nz - 1], gate_recv.at[2])
-    total = gate_all[at_mine, :]
-    for j in range(1, nz):
-        total = total + pieces[lax.rem(z + j, nz)]
-    sums[...] = total
-    full[at_mine, :] = total
-
-    def back_to_column(j, carry):
-        to = place(lax.rem(z + j, nz), x, y, core)
-        remote(sums, full.at[at_mine, :], gate_send.at[3], gate_recv.at[3], to).start()
+    lax.fori_loop(0, QB // TILE, forward_b, 0)
+    share_gate()
+
+    def backward_b(step, carry):
+        t = lax.rem(turn + step, QB // TILE)
+        backward_tile(t, kv_b, qg_b, acc_b, res_b, exps, scaled, dots)
+
+        @pl.when(jnp.logical_and(step == 0, core == 1))
+        def _():
+            to_column(1)
+
+        @pl.when(jnp.logical_and(step == 2, core == 0))
+        def _():
+            go_along_x(0)
+
+        @pl.when(step == 1)
+        def _():
+            ahead_a.wait()
+            for i, s in ((0, SCALE), (1, 1.0)):
+                first = acc_a[i, WINDOW : WINDOW + SPAN, :] * s + ra_a[i].astype(F32)
+                dkv_a[i, 0:SPAN, :] = first.astype(BF16)
+
+            def give_first(i, carry):
+                give_whole(dkv_a, out_kv, i, 1)
+                return carry
+
+            lax.fori_loop(0, SPAN // BLOCK, give_first, 0)
+
+        @pl.when(jnp.logical_and(step == 2, core == 1))
+        def _():
+            back_to_column()
+
+        for j in range(TILE // BLOCK):
+            give_shared(res_b, out_mq, t * (TILE // BLOCK) + j, 0)
+
         return carry
 
-    lax.fori_loop(1, nz, back_to_column, 0)
-
-    ahead_a.wait()
+    lax.fori_loop(0, QB // TILE, backward_b, 0)
+
     for i, s in ((0, SCALE), (1, 1.0)):
-        first = acc_a[i, WINDOW : WINDOW + SPAN, :] * s + ra_a[i].astype(F32)
-        dkv_a[i, 0:SPAN, :] = first.astype(BF16)
-    def give_first(i, carry):
-        give_whole(dkv_a, out_kv, i, 1)
-        return carry
-
-    lax.fori_loop(0, SPAN // BLOCK, give_first, 0)
-
-    took(full.at[0 : (nz - 1) * piece, :], gate_recv.at[3])
-    split = whole_head(0, 4) * DH
-    half_rows = DH // 2
-    low_rows = pl.ds(pl.multiple_of(x_lo * half_rows, half_rows), half_rows)
-    row_a = pl.ds(pl.multiple_of(y * 4 * DH, DH), 4 * DH)
-    row_b = pl.ds(pl.multiple_of(split + y * 2 * DH, DH), 2 * DH)
-    full_low[...] = full[...].astype(BF16)
-
-    def spread_gate(mine, row, one, three, all_rows, theirs):
-        for jx in range(1, 4):
-            to = place(z, lax.rem(x + jx, 4), y, core)
-            remote(mine[0], mine[1], gate_send.at[4], gate_recv.at[4], to).start()
-        took(one, gate_recv.at[4])
-        for jy in range(1, 4):
-            to = place(z, x, lax.rem(y + jy, 4), core)
-            remote(row, row, gate_send.at[5], gate_recv.at[5], to).start()
-        took(three, gate_recv.at[5])
-        remote(all_rows, all_rows, gate_send.at[6], gate_recv.at[6], other_core).start()
-        took(theirs, gate_recv.at[6])
-        took(one, gate_send.at[4])
-        took(three, gate_send.at[5])
-        took(all_rows, gate_send.at[6])
-
-    whole = gate_buf.at[:, 0:split]
-    shared = gate_buf.at[:, split:]
+        sb_b[i] = (acc_b[i, 0:WINDOW, :] * s).astype(BF16)
+        sa_b[i] = (acc_b[i, WINDOW + QB :, :] * s).astype(BF16)
+    behind_b.start()
+    ahead_b.start()
 
     @pl.when(core == 0)
     def _():
-        at = cols(whole_head(x, y))
-        gate_buf[:, at] = full_low[...]
-        spread_gate(
-            (full_low, gate_buf.at[:, at]), gate_buf.at[:, row_a],
-            gate_buf.at[:, 0 : 3 * DH], gate_buf.at[:, 0 : 12 * DH], whole, shared,
-        )
+        go_along_y(0)
 
     @pl.when(core == 1)
     def _():
-        at = cols(shared_head(x, y))
-        gate_buf[low_rows, at] = full_low[low_rows, :]
-        spread_gate(
-            (full_low.at[low_rows, :], gate_buf.at[low_rows, at]), gate_buf.at[:, row_b],
-            gate_buf.at[0:half_rows, 0 : 3 * DH], gate_buf.at[:, 0 : 6 * DH], shared, whole,
-        )
+        go_along_x(1)
+
+    finish_b()
+
+    @pl.when(core == 0)
+    def _():
+        go_across(0)
+
+    @pl.when(core == 1)
+    def _():
+        go_along_y(1)
+
+    @pl.when(core == 0)
+    def _():
+        last(0)
+
+    @pl.when(core == 1)
+    def _():
+        go_across(1)
+        last(1)
 
     took(pieces.at[0 : nz - 1], gate_send.at[2])
     took(full.at[0 : (nz - 1) * piece, :], gate_send.at[3])
@@ -569,10 +698,11 @@
             wide(QA // TILE, SLAB, TILE), wide(QB // TILE, SLAB, TILE),
             wide(QA, DH), wide(QB, DH), low(levels, QA), low(levels, QB),
             wide(2, rows_a, DH), wide(2, rows_b, DH),
+            low(QB // TILE, SLAB, TILE), low(QB // TILE, DH, TILE), wide(QB // TILE, 1, TILE),
             low(2, QA, DH), low(2, QB, DH), low(2, QA, DH), low(2, QB, DH),
             low(2, WINDOW, DH), low(2, WINDOW, DH), low(2, SPAN, DH), low(2, SPAN, DH),
             low(2, WINDOW, DH), low(2, WINDOW, DH), low(2, SPAN, DH), low(2, SPAN, DH),
-            wide(2, levels, DH), wide(levels, DH), wide(levels, DH), wide(levels, DH),
+            wide(2, levels, DH), wide(3, levels, DH), wide(levels, DH), wide(levels, DH),
             wide(nz, piece, DH), wide(piece, DH), wide(levels, DH), low(levels, DH),
             sems(6), sems(4), sems(4), sems(4), sems(4), sems(4), sems(4), sems(4), sems(2),
             sems(7), sems(7),

time: 108 us -> 111 us (1.028)
  Pallas kernels: 102 us -> 105 us
    pallas_call x1, Pallas kernels: 102 us -> 105 us  [fused(): pl.pallas_call(functools.partial(kernel, nz), out_shape=[jax.ShapeDtypeSt...]
where the time goes in v4:
time: 111 us; the launch traced here: 110 us
  Pallas kernels  105 us (95%)
  local copies, waits for them, and re-layouts  3.63 us (3%)
  other arithmetic  1.3 us (1%)
    pallas_call x1, Pallas kernels, fused(): pl.pallas_call(functools.partial(kernel, nz), out_shape=[jax.ShapeDtypeSt...  105 us
    squeeze x1, local copies, waits for them, and re-layouts, per_device(): return (mq[0], mq[1], kv[0], kv[1], gate_low.astype(F32))  3.63 us

profile of v4, /device:TPU:1, one launch (start us, length us, event | category | flops | bytes accessed | tf_op | source)
XLA Modules:
  0.0 110.5 jit_solution(17974157198534131821)
XLA Ops:
  0.6 104.9 %shard_map.119 = (bf16[2,128,3072]{2,1,0:T(8,128)(2,1)}, bf16[2,128,3072]{2,1,0:T(8,128)(2,1)}, bf16[128,3072]{1,0:T(8,128)(2,1)}) custom-call(s32[256,128]{1,0:T(8,128)} %bitcast.10, s32[1,192]{1,0:T(1,128)} %bitcast.11, s32[192,192]{1,0:T(8,128)} %mask_ref.1, f32[128,3072]{1,0:T(8,128)} %tab_ref.1, bf16[128,3072]{1,0:T(8,128)(2,1)} %q_ref.1, ...), custom_call_target="tpu_custom_call" | custom-call | tf_op jit(solution)/shard_map/pallas_call | solution.py:684
  105.5 0.0 copy-start
  105.5 3.6 %slice_bitcast_fusion = (bf16[128,3072]{1,0:T(8,128)(2,1)}, bf16[128,3072]{1,0:T(8,128)(2,1)}, bf16[128,3072]{1,0:T(8,128)(2,1)}, bf16[128,3072]{1,0:T(8,128)(2,1)}) fusion(bf16[2,128,3072]{2,1,0:T(8,128)(2,1)} %get-tuple-element.9, bf16[2,128,3072]{2,1,0:T(8,128)(2,1)} %get-tuple-element.8), kind=kLoop, calls=%fused_computation | loop fusion | bytes 6291456 | tf_op jit(solution)/shard_map/squeeze | solution.py:722
  109.2 0.0 copy-done
  109.2 1.3 %convert_element_type.3 = f32[128,3072]{1,0:T(8,128)} convert(bf16[128,3072]{1,0:T(8,128)(2,1)S(1)} %copy-done) | non-fusion elementwise | flops 393216 | bytes 2359296 | tf_op jit(solution)/shard_map/convert_element_type | solution.py:722
Async XLA Ops:
  105.5 3.6 %copy-start = (bf16[128,3072]{1,0:T(8,128)(2,1)S(1)}, bf16[128,3072]{1,0:T(8,128)(2,1)}, u32[]{:S(2)}) copy-start(bf16[128,3072]{1,0:T(8,128)(2,1)} %get-tuple-element.10) | copy-start | bytes 2359300

commit v5 on v3

--- a/solution.py
+++ b/solution.py
@@ -463,24 +463,17 @@
     split = whole_head(0, 4) * DH
     half_rows = DH // 2
     low_rows = pl.ds(pl.multiple_of(x_lo * half_rows, half_rows), half_rows)
-    row_a = pl.ds(pl.multiple_of(y * 4 * DH, DH), 4 * DH)
-    row_b = pl.ds(pl.multiple_of(split + y * 2 * DH, DH), 2 * DH)
     full_low[...] = full[...].astype(BF16)
 
-    def spread_gate(mine, row, one, three, all_rows, theirs):
-        for jx in range(1, 4):
-            to = place(z, lax.rem(x + jx, 4), y, core)
-            remote(mine[0], mine[1], gate_send.at[4], gate_recv.at[4], to).start()
-        took(one, gate_recv.at[4])
-        for jy in range(1, 4):
-            to = place(z, x, lax.rem(y + jy, 4), core)
-            remote(row, row, gate_send.at[5], gate_recv.at[5], to).start()
-        took(three, gate_recv.at[5])
-        remote(all_rows, all_rows, gate_send.at[6], gate_recv.at[6], other_core).start()
+    def spread_gate(src, dst, fifteen, mine, theirs):
+        for jx, jy in FAR_FIRST[:-1]:
+            to = place(z, lax.rem(x + jx, 4), lax.rem(y + jy, 4), core)
+            remote(src, dst, gate_send.at[4], gate_recv.at[4], to).start()
+        took(fifteen, gate_recv.at[4])
+        remote(mine, mine, gate_send.at[6], gate_recv.at[6], other_core).start()
         took(theirs, gate_recv.at[6])
-        took(one, gate_send.at[4])
-        took(three, gate_send.at[5])
-        took(all_rows, gate_send.at[6])
+        took(fifteen, gate_send.at[4])
+        took(mine, gate_send.at[6])
 
     whole = gate_buf.at[:, 0:split]
     shared = gate_buf.at[:, split:]
@@ -489,18 +482,15 @@
     def _():
         at = cols(whole_head(x, y))
         gate_buf[:, at] = full_low[...]
-        spread_gate(
-            (full_low, gate_buf.at[:, at]), gate_buf.at[:, row_a],
-            gate_buf.at[:, 0 : 3 * DH], gate_buf.at[:, 0 : 12 * DH], whole, shared,
-        )
+        spread_gate(full_low, gate_buf.at[:, at], gate_buf.at[:, 0 : 15 * DH], whole, shared)
 
     @pl.when(core == 1)
     def _():
         at = cols(shared_head(x, y))
         gate_buf[low_rows, at] = full_low[low_rows, :]
         spread_gate(
-            (full_low.at[low_rows, :], gate_buf.at[low_rows, at]), gate_buf.at[:, row_b],
-            gate_buf.at[0:half_rows, 0 : 3 * DH], gate_buf.at[:, 0 : 6 * DH], shared, whole,
+            full_low.at[low_rows, :], gate_buf.at[low_rows, at],
+            gate_buf.at[0:half_rows, 0 : 15 * DH], shared, whole,
         )
 
     took(pieces.at[0 : nz - 1], gate_send.at[2])

time: 108 us -> 107 us (level)
  no operation moved by 1% of the time
where the time goes in v5:
time: 107 us
  Pallas kernels  101 us (94%)
  local copies, waits for them, and re-layouts  3.63 us (3%)
  other arithmetic  1.3 us (1%)
    pallas_call x1, Pallas kernels, fused(): pl.pallas_call(functools.partial(kernel, nz), out_shape=[jax.ShapeDtypeSt...  101 us
    squeeze x1, local copies, waits for them, and re-layouts, per_device(): return (mq[0], mq[1], kv[0], kv[1], gate_low.astype(F32))  3.63 us

profile of v5, /device:TPU:1, one launch (start us, length us, event | category | flops | bytes accessed | tf_op | source)
XLA Modules:
  0.0 106.8 jit_solution(5632970013111386982)
XLA Ops:
  0.6 101.2 %shard_map.119 = (bf16[2,128,3072]{2,1,0:T(8,128)(2,1)}, bf16[2,128,3072]{2,1,0:T(8,128)(2,1)}, bf16[128,3072]{1,0:T(8,128)(2,1)}) custom-call(s32[256,128]{1,0:T(8,128)} %bitcast.10, s32[1,192]{1,0:T(1,128)} %bitcast.11, s32[192,192]{1,0:T(8,128)} %mask_ref.1, f32[128,3072]{1,0:T(8,128)} %tab_ref.1, bf16[128,3072]{1,0:T(8,128)(2,1)} %q_ref.1, ...), custom_call_target="tpu_custom_call" | custom-call | tf_op jit(solution)/shard_map/pallas_call | solution.py:545
  101.9 0.0 copy-start
  101.9 3.6 %slice_bitcast_fusion = (bf16[128,3072]{1,0:T(8,128)(2,1)}, bf16[128,3072]{1,0:T(8,128)(2,1)}, bf16[128,3072]{1,0:T(8,128)(2,1)}, bf16[128,3072]{1,0:T(8,128)(2,1)}) fusion(bf16[2,128,3072]{2,1,0:T(8,128)(2,1)} %get-tuple-element.9, bf16[2,128,3072]{2,1,0:T(8,128)(2,1)} %get-tuple-element.8), kind=kLoop, calls=%fused_computation | loop fusion | bytes 6291456 | tf_op jit(solution)/shard_map/squeeze | solution.py:582
  105.5 0.0 copy-done
  105.5 1.3 %convert_element_type.3 = f32[128,3072]{1,0:T(8,128)} convert(bf16[128,3072]{1,0:T(8,128)(2,1)S(1)} %copy-done) | non-fusion elementwise | flops 393216 | bytes 2359296 | tf_op jit(solution)/shard_map/convert_element_type | solution.py:582
Async XLA Ops:
  101.9 3.6 %copy-start = (bf16[128,3072]{1,0:T(8,128)(2,1)S(1)}, bf16[128,3072]{1,0:T(8,128)(2,1)}, u32[]{:S(2)}) copy-start(bf16[128,3072]{1,0:T(8,128)(2,1)} %get-tuple-element.10) | copy-start | bytes 2359300
